TPU v7x, 512 devices: a whole 4x4x16 slice. The times are simulated.
512 devices in a mesh: ctx: 32 (over x_hi, z), head: 8 (over y, x_lo), dp: 2 (over core).
Axes of the slice: x: 4 (x_hi: 2, x_lo: 2; x = x_hi * 2 + x_lo), y: 4, z: 16, core: 2. Of those that a mesh axis runs over, the one named last changes fastest.
Arguments:
- queries: bfloat16 [8192, 3072], P(('dp', 'ctx'), 'head'), parts along dimension 0, may hold values from -5.5 to 5.5
- keys: bfloat16 [8192, 3072], P(('dp', 'ctx'), 'head'), parts along dimension 0, may hold values from -5.5 to 5.5
- values: bfloat16 [8192, 3072], P(('dp', 'ctx'), 'head'), parts along dimension 0, may hold values from -6 to 6
- tan_queries: bfloat16 [8192, 3072], P(('dp', 'ctx'), 'head'), parts along dimension 0, may hold values from -6 to 6
- tan_keys: bfloat16 [8192, 3072], P(('dp', 'ctx'), 'head'), parts along dimension 0, may hold values from -6 to 6
- tan_values: bfloat16 [8192, 3072], P(('dp', 'ctx'), 'head'), parts along dimension 0, may hold values from -6 to 6
- out_weight: bfloat16 [3072, 5120], P('head'), may hold values from -0.15625 to 0.15625
- clip_lengths: int32 [32], P('dp'), parts along dimension 0, may hold values from 1 to 1024, 4096 in all
- stretch_order: int32 [128], P('dp'), parts along dimension 0, may hold values from 0 to 63, each once
Outputs:
- attended: bfloat16 [8192, 5120], P(('dp', 'ctx'), 'head'), parts along dimension 0
- tan_attended: bfloat16 [8192, 5120], P(('dp', 'ctx'), 'head'), parts along dimension 0
There are 2 independent parts, one for each index of `dp`. A program takes and returns all parts, laid end to end along the dimension named above; an argument that names none is the same for every part. Nothing has to cross between parts.
Inputs may be any that keep to these rules, and one draw needn't show every extreme that they name: `stretch_order`: each is a permutation. `clip_lengths`: they sum to 4096; the longest is 1024.
All inputs are finite; a program needn't handle non-finite values.
Results may differ from a plain program's by a relative error of at most 0.02.
Values may be sent and summed in bfloat16 or wider, within the bound.
A program may use at most 64 MiB of HBM per device.

v0:
```python
import jax
import jax.numpy as jnp
from jax import lax
from jax.sharding import PartitionSpec as P

HDIM = 128


def shifted(value, axis, steps):
    count = lax.axis_size(axis)
    pairs = [(source, (source + steps) % count) for source in range(count)]
    return lax.ppermute(value, axis, pairs)


def segment_ids(row_ids, stretch_order, clip_ends, half_rows):
    stretch = row_ids // half_rows
    table = stretch[:, None] == jnp.arange(stretch_order.shape[0], dtype=jnp.int32)[None, :]
    anchor = (
        jnp.sum(jnp.where(table, stretch_order[None, :], 0), axis=1) * half_rows
        + row_ids % half_rows
    )
    return jnp.sum((clip_ends[None, :] <= anchor[:, None]).astype(jnp.int32), axis=1)


def local(
    queries,
    keys,
    values,
    tan_queries,
    tan_keys,
    tan_values,
    out_weight,
    clip_lengths,
    stretch_order,
):
    tok_rows = queries.shape[0]
    width = queries.shape[1]
    local_heads = width // HDIM
    half_rows = tok_rows // 2
    ctx_size = lax.axis_size("ctx")
    my_index = lax.axis_index("ctx")
    clip_ends = jnp.cumsum(clip_lengths)
    own_rows = my_index * tok_rows + jnp.arange(tok_rows, dtype=jnp.int32)
    own_seg = segment_ids(own_rows, stretch_order, clip_ends, half_rows)
    query_heads = queries.reshape(tok_rows, local_heads, HDIM)
    tan_query_heads = tan_queries.reshape(tok_rows, local_heads, HDIM)
    score_scale = 1.0 / HDIM**0.5

    def attend(state_now, blocks, first_row):
        span = blocks.shape[1]
        block_rows = first_row + jnp.arange(span, dtype=jnp.int32)
        block_seg = segment_ids(block_rows, stretch_order, clip_ends, half_rows)
        allowed = jnp.logical_and(own_seg[:, None] == block_seg[None, :], True)
        running_max, total, tan_total, accum, tan_accum = state_now
        key_heads = blocks[0].reshape(span, local_heads, HDIM)
        value_heads = blocks[1].reshape(span, local_heads, HDIM)
        tan_key_heads = blocks[2].reshape(span, local_heads, HDIM)
        tan_value_heads = blocks[3].reshape(span, local_heads, HDIM)
        scores = (
            jnp.einsum("qhd,khd->hqk", query_heads, key_heads, preferred_element_type=jnp.float32)
            * score_scale
        )
        tan_scores = (
            jnp.einsum(
                "qhd,khd->hqk", tan_query_heads, key_heads, preferred_element_type=jnp.float32
            )
            + jnp.einsum(
                "qhd,khd->hqk", query_heads, tan_key_heads, preferred_element_type=jnp.float32
            )
        ) * score_scale
        masked = jnp.where(allowed[None], scores, -1e30)
        new_max = jnp.maximum(running_max, jnp.max(masked, axis=2))
        weights = jnp.where(allowed[None], jnp.exp(masked - new_max[..., None]), 0.0)
        rescale = jnp.exp(running_max - new_max)
        products = weights * tan_scores
        total = rescale * total + jnp.sum(weights, axis=2)
        tan_total = rescale * tan_total + jnp.sum(products, axis=2)
        weights_b = weights.astype(jnp.bfloat16)
        products_b = products.astype(jnp.bfloat16)
        accum = rescale[..., None] * accum + jnp.einsum(
            "hqk,khd->hqd", weights_b, value_heads, preferred_element_type=jnp.float32
        )
        tan_accum = (
            rescale[..., None] * tan_accum
            + jnp.einsum(
                "hqk,khd->hqd", products_b, value_heads, preferred_element_type=jnp.float32
            )
            + jnp.einsum(
                "hqk,khd->hqd", weights_b, tan_value_heads, preferred_element_type=jnp.float32
            )
        )
        return (new_max, total, tan_total, accum, tan_accum)

    block = jnp.stack([keys, values, tan_keys, tan_values])
    initial = (
        jnp.full((local_heads, tok_rows), -1e30, jnp.float32),
        jnp.zeros((local_heads, tok_rows), jnp.float32),
        jnp.zeros((local_heads, tok_rows), jnp.float32),
        jnp.zeros((local_heads, tok_rows, HDIM), jnp.float32),
        jnp.zeros((local_heads, tok_rows, HDIM), jnp.float32),
    )

    def one_side(hop_index, packed):
        state_now, moving = packed
        moving = shifted(moving, "ctx", 1)
        source = (my_index - hop_index - 1) % ctx_size
        return (attend(state_now, moving, source * tok_rows), moving)

    start_state = attend(initial, block, my_index * tok_rows)
    state_end = lax.fori_loop(0, ctx_size - 1, one_side, (start_state, block))[0]
    running_max, total, tan_total, accum, tan_accum = state_end
    primal = accum / total[..., None]
    tangent = tan_accum / total[..., None] - (tan_total / total)[..., None] * primal
    primal_rows = primal.transpose(1, 0, 2).reshape(tok_rows, width)
    tangent_rows = tangent.transpose(1, 0, 2).reshape(tok_rows, width)
    heads_out = jnp.stack([primal_rows, tangent_rows]).astype(jnp.bfloat16)
    terms = jnp.einsum("srw,wd->srd", heads_out, out_weight, preferred_element_type=jnp.float32)
    summed = lax.psum_scatter(
        terms.astype(jnp.bfloat16), "head", scatter_dimension=2, tiled=True
    ).astype(jnp.float32)
    return (summed[0].astype(jnp.bfloat16), summed[1].astype(jnp.bfloat16))


def solution(mesh):
    placed = (
        P(("dp", "ctx"), "head"),
        P(("dp", "ctx"), "head"),
        P(("dp", "ctx"), "head"),
        P(("dp", "ctx"), "head"),
        P(("dp", "ctx"), "head"),
        P(("dp", "ctx"), "head"),
        P("head", None),
        P("dp"),
        P("dp"),
    )
    return jax.shard_map(
        local,
        mesh=mesh,
        in_specs=placed,
        out_specs=(P(("dp", "ctx"), "head"), P(("dp", "ctx"), "head")),
        check_vma=False,
    )
```

profile of v0, /device:TPU:1, one launch (start us, length us, event | category | flops | bytes accessed | tf_op | source)
XLA Modules:
  0.0 611.7 jit_solution(4860993457424359788)
XLA Ops:
  17.1 480.5 %while.26 = (s32[]{:T(128)}, f32[3,128]{1,0:T(4,128)S(1)}, f32[3,128]{1,0:T(4,128)S(1)}, f32[3,128]{1,0:T(4,128)S(1)}, f32[3,128,128]{2,1,0:T(8,128)S(1)}, /*ind...) while((s32[]{:T(128)}, f32[3,128]{1,0:T(4,128)S(1)}, ...), condition=%wide.region_12.13_spmd, body=%wide.region_6.12_spmd.sunk | while | flops 76728976 | bytes 6923438 | solution.py:110
  17.1 4.4 collective-permute-start
  21.8 18.5 %collective-permute-done = bf16[4,128,384]{1,2,0:T(8,128)(2,1)S(1)} collective-permute-done((bf16[4,128,384]{1,2,0:T(8,128)(2,1)S(1)}, bf16[4,128,384]{1,2,0:T(8,128)(2,1)S(1)}, u32[]{:S(2)}, u32[]{:S(2)}) %collective-permute-start) | collective-permute-done | bytes 393248 | tf_op jit(solution)/shard_map/while/body/eval_jaxpr/ppermute | solution.py:12
  42.0 1.9 collective-permute-start
  44.3 12.6 %collective-permute-done = bf16[4,128,384]{1,2,0:T(8,128)(2,1)S(1)} collective-permute-done((bf16[4,128,384]{1,2,0:T(8,128)(2,1)S(1)}, bf16[4,128,384]{1,2,0:T(8,128)(2,1)S(1)}, u32[]{:S(2)}, u32[]{:S(2)}) %collective-permute-start) | collective-permute-done | bytes 393248 | tf_op jit(solution)/shard_map/while/body/eval_jaxpr/ppermute | solution.py:12
  58.6 1.9 collective-permute-start
  60.9 11.7 %collective-permute-done = bf16[4,128,384]{1,2,0:T(8,128)(2,1)S(1)} collective-permute-done((bf16[4,128,384]{1,2,0:T(8,128)(2,1)S(1)}, bf16[4,128,384]{1,2,0:T(8,128)(2,1)S(1)}, u32[]{:S(2)}, u32[]{:S(2)}) %collective-permute-start) | collective-permute-done | bytes 393248 | tf_op jit(solution)/shard_map/while/body/eval_jaxpr/ppermute | solution.py:12
  74.3 1.9 collective-permute-start
  76.5 10.8 %collective-permute-done = bf16[4,128,384]{1,2,0:T(8,128)(2,1)S(1)} collective-permute-done((bf16[4,128,384]{1,2,0:T(8,128)(2,1)S(1)}, bf16[4,128,384]{1,2,0:T(8,128)(2,1)S(1)}, u32[]{:S(2)}, u32[]{:S(2)}) %collective-permute-start) | collective-permute-done | bytes 393248 | tf_op jit(solution)/shard_map/while/body/eval_jaxpr/ppermute | solution.py:12
  89.0 1.9 collective-permute-start
  91.3 9.9 %collective-permute-done = bf16[4,128,384]{1,2,0:T(8,128)(2,1)S(1)} collective-permute-done((bf16[4,128,384]{1,2,0:T(8,128)(2,1)S(1)}, bf16[4,128,384]{1,2,0:T(8,128)(2,1)S(1)}, u32[]{:S(2)}, u32[]{:S(2)}) %collective-permute-start) | collective-permute-done | bytes 393248 | tf_op jit(solution)/shard_map/while/body/eval_jaxpr/ppermute | solution.py:12
  102.8 1.9 collective-permute-start
  105.1 9.9 %collective-permute-done = bf16[4,128,384]{1,2,0:T(8,128)(2,1)S(1)} collective-permute-done((bf16[4,128,384]{1,2,0:T(8,128)(2,1)S(1)}, bf16[4,128,384]{1,2,0:T(8,128)(2,1)S(1)}, u32[]{:S(2)}, u32[]{:S(2)}) %collective-permute-start) | collective-permute-done | bytes 393248 | tf_op jit(solution)/shard_map/while/body/eval_jaxpr/ppermute | solution.py:12
  116.7 1.9 collective-permute-start
  118.9 9.9 %collective-permute-done = bf16[4,128,384]{1,2,0:T(8,128)(2,1)S(1)} collective-permute-done((bf16[4,128,384]{1,2,0:T(8,128)(2,1)S(1)}, bf16[4,128,384]{1,2,0:T(8,128)(2,1)S(1)}, u32[]{:S(2)}, u32[]{:S(2)}) %collective-permute-start) | collective-permute-done | bytes 393248 | tf_op jit(solution)/shard_map/while/body/eval_jaxpr/ppermute | solution.py:12
  130.5 1.9 collective-permute-start
  132.8 9.9 %collective-permute-done = bf16[4,128,384]{1,2,0:T(8,128)(2,1)S(1)} collective-permute-done((bf16[4,128,384]{1,2,0:T(8,128)(2,1)S(1)}, bf16[4,128,384]{1,2,0:T(8,128)(2,1)S(1)}, u32[]{:S(2)}, u32[]{:S(2)}) %collective-permute-start) | collective-permute-done | bytes 393248 | tf_op jit(solution)/shard_map/while/body/eval_jaxpr/ppermute | solution.py:12
  144.3 1.9 collective-permute-start
  146.6 9.9 %collective-permute-done = bf16[4,128,384]{1,2,0:T(8,128)(2,1)S(1)} collective-permute-done((bf16[4,128,384]{1,2,0:T(8,128)(2,1)S(1)}, bf16[4,128,384]{1,2,0:T(8,128)(2,1)S(1)}, u32[]{:S(2)}, u32[]{:S(2)}) %collective-permute-start) | collective-permute-done | bytes 393248 | tf_op jit(solution)/shard_map/while/body/eval_jaxpr/ppermute | solution.py:12
  158.2 1.9 collective-permute-start
  160.4 9.9 %collective-permute-done = bf16[4,128,384]{1,2,0:T(8,128)(2,1)S(1)} collective-permute-done((bf16[4,128,384]{1,2,0:T(8,128)(2,1)S(1)}, bf16[4,128,384]{1,2,0:T(8,128)(2,1)S(1)}, u32[]{:S(2)}, u32[]{:S(2)}) %collective-permute-start) | collective-permute-done | bytes 393248 | tf_op jit(solution)/shard_map/while/body/eval_jaxpr/ppermute | solution.py:12
  172.0 1.9 collective-permute-start
  174.3 10.5 %collective-permute-done = bf16[4,128,384]{1,2,0:T(8,128)(2,1)S(1)} collective-permute-done((bf16[4,128,384]{1,2,0:T(8,128)(2,1)S(1)}, bf16[4,128,384]{1,2,0:T(8,128)(2,1)S(1)}, u32[]{:S(2)}, u32[]{:S(2)}) %collective-permute-start) | collective-permute-done | bytes 393248 | tf_op jit(solution)/shard_map/while/body/eval_jaxpr/ppermute | solution.py:12
  186.4 1.9 collective-permute-start
  188.7 11.5 %collective-permute-done = bf16[4,128,384]{1,2,0:T(8,128)(2,1)S(1)} collective-permute-done((bf16[4,128,384]{1,2,0:T(8,128)(2,1)S(1)}, bf16[4,128,384]{1,2,0:T(8,128)(2,1)S(1)}, u32[]{:S(2)}, u32[]{:S(2)}) %collective-permute-start) | collective-permute-done | bytes 393248 | tf_op jit(solution)/shard_map/while/body/eval_jaxpr/ppermute | solution.py:12
  201.9 1.9 collective-permute-start
  204.2 12.6 %collective-permute-done = bf16[4,128,384]{1,2,0:T(8,128)(2,1)S(1)} collective-permute-done((bf16[4,128,384]{1,2,0:T(8,128)(2,1)S(1)}, bf16[4,128,384]{1,2,0:T(8,128)(2,1)S(1)}, u32[]{:S(2)}, u32[]{:S(2)}) %collective-permute-start) | collective-permute-done | bytes 393248 | tf_op jit(solution)/shard_map/while/body/eval_jaxpr/ppermute | solution.py:12
  218.5 1.9 collective-permute-start
  220.7 13.7 %collective-permute-done = bf16[4,128,384]{1,2,0:T(8,128)(2,1)S(1)} collective-permute-done((bf16[4,128,384]{1,2,0:T(8,128)(2,1)S(1)}, bf16[4,128,384]{1,2,0:T(8,128)(2,1)S(1)}, u32[]{:S(2)}, u32[]{:S(2)}) %collective-permute-start) | collective-permute-done | bytes 393248 | tf_op jit(solution)/shard_map/while/body/eval_jaxpr/ppermute | solution.py:12
  236.1 1.9 collective-permute-start
  238.4 13.6 %collective-permute-done = bf16[4,128,384]{1,2,0:T(8,128)(2,1)S(1)} collective-permute-done((bf16[4,128,384]{1,2,0:T(8,128)(2,1)S(1)}, bf16[4,128,384]{1,2,0:T(8,128)(2,1)S(1)}, u32[]{:S(2)}, u32[]{:S(2)}) %collective-permute-start) | collective-permute-done | bytes 393248 | tf_op jit(solution)/shard_map/while/body/eval_jaxpr/ppermute | solution.py:12
  253.7 1.9 collective-permute-start
  255.9 12.6 %collective-permute-done = bf16[4,128,384]{1,2,0:T(8,128)(2,1)S(1)} collective-permute-done((bf16[4,128,384]{1,2,0:T(8,128)(2,1)S(1)}, bf16[4,128,384]{1,2,0:T(8,128)(2,1)S(1)}, u32[]{:S(2)}, u32[]{:S(2)}) %collective-permute-start) | collective-permute-done | bytes 393248 | tf_op jit(solution)/shard_map/while/body/eval_jaxpr/ppermute | solution.py:12
  270.3 1.9 collective-permute-start
  272.5 11.7 %collective-permute-done = bf16[4,128,384]{1,2,0:T(8,128)(2,1)S(1)} collective-permute-done((bf16[4,128,384]{1,2,0:T(8,128)(2,1)S(1)}, bf16[4,128,384]{1,2,0:T(8,128)(2,1)S(1)}, u32[]{:S(2)}, u32[]{:S(2)}) %collective-permute-start) | collective-permute-done | bytes 393248 | tf_op jit(solution)/shard_map/while/body/eval_jaxpr/ppermute | solution.py:12
  285.9 1.9 collective-permute-start
  288.2 10.8 %collective-permute-done = bf16[4,128,384]{1,2,0:T(8,128)(2,1)S(1)} collective-permute-done((bf16[4,128,384]{1,2,0:T(8,128)(2,1)S(1)}, bf16[4,128,384]{1,2,0:T(8,128)(2,1)S(1)}, u32[]{:S(2)}, u32[]{:S(2)}) %collective-permute-start) | collective-permute-done | bytes 393248 | tf_op jit(solution)/shard_map/while/body/eval_jaxpr/ppermute | solution.py:12
  300.7 1.9 collective-permute-start
  302.9 9.9 %collective-permute-done = bf16[4,128,384]{1,2,0:T(8,128)(2,1)S(1)} collective-permute-done((bf16[4,128,384]{1,2,0:T(8,128)(2,1)S(1)}, bf16[4,128,384]{1,2,0:T(8,128)(2,1)S(1)}, u32[]{:S(2)}, u32[]{:S(2)}) %collective-permute-start) | collective-permute-done | bytes 393248 | tf_op jit(solution)/shard_map/while/body/eval_jaxpr/ppermute | solution.py:12
  314.5 1.9 collective-permute-start
  316.8 9.9 %collective-permute-done = bf16[4,128,384]{1,2,0:T(8,128)(2,1)S(1)} collective-permute-done((bf16[4,128,384]{1,2,0:T(8,128)(2,1)S(1)}, bf16[4,128,384]{1,2,0:T(8,128)(2,1)S(1)}, u32[]{:S(2)}, u32[]{:S(2)}) %collective-permute-start) | collective-permute-done | bytes 393248 | tf_op jit(solution)/shard_map/while/body/eval_jaxpr/ppermute | solution.py:12
  328.3 1.9 collective-permute-start
  330.6 9.9 %collective-permute-done = bf16[4,128,384]{1,2,0:T(8,128)(2,1)S(1)} collective-permute-done((bf16[4,128,384]{1,2,0:T(8,128)(2,1)S(1)}, bf16[4,128,384]{1,2,0:T(8,128)(2,1)S(1)}, u32[]{:S(2)}, u32[]{:S(2)}) %collective-permute-start) | collective-permute-done | bytes 393248 | tf_op jit(solution)/shard_map/while/body/eval_jaxpr/ppermute | solution.py:12
  342.2 1.9 collective-permute-start
  344.4 9.9 %collective-permute-done = bf16[4,128,384]{1,2,0:T(8,128)(2,1)S(1)} collective-permute-done((bf16[4,128,384]{1,2,0:T(8,128)(2,1)S(1)}, bf16[4,128,384]{1,2,0:T(8,128)(2,1)S(1)}, u32[]{:S(2)}, u32[]{:S(2)}) %collective-permute-start) | collective-permute-done | bytes 393248 | tf_op jit(solution)/shard_map/while/body/eval_jaxpr/ppermute | solution.py:12
  356.0 1.9 collective-permute-start
  358.3 9.9 %collective-permute-done = bf16[4,128,384]{1,2,0:T(8,128)(2,1)S(1)} collective-permute-done((bf16[4,128,384]{1,2,0:T(8,128)(2,1)S(1)}, bf16[4,128,384]{1,2,0:T(8,128)(2,1)S(1)}, u32[]{:S(2)}, u32[]{:S(2)}) %collective-permute-start) | collective-permute-done | bytes 393248 | tf_op jit(solution)/shard_map/while/body/eval_jaxpr/ppermute | solution.py:12
  369.8 1.9 collective-permute-start
  372.1 9.9 %collective-permute-done = bf16[4,128,384]{1,2,0:T(8,128)(2,1)S(1)} collective-permute-done((bf16[4,128,384]{1,2,0:T(8,128)(2,1)S(1)}, bf16[4,128,384]{1,2,0:T(8,128)(2,1)S(1)}, u32[]{:S(2)}, u32[]{:S(2)}) %collective-permute-start) | collective-permute-done | bytes 393248 | tf_op jit(solution)/shard_map/while/body/eval_jaxpr/ppermute | solution.py:12
  383.7 1.9 collective-permute-start
  385.9 10.5 %collective-permute-done = bf16[4,128,384]{1,2,0:T(8,128)(2,1)S(1)} collective-permute-done((bf16[4,128,384]{1,2,0:T(8,128)(2,1)S(1)}, bf16[4,128,384]{1,2,0:T(8,128)(2,1)S(1)}, u32[]{:S(2)}, u32[]{:S(2)}) %collective-permute-start) | collective-permute-done | bytes 393248 | tf_op jit(solution)/shard_map/while/body/eval_jaxpr/ppermute | solution.py:12
  400.3 11.5 %collective-permute-done = bf16[4,128,384]{1,2,0:T(8,128)(2,1)S(1)} collective-permute-done((bf16[4,128,384]{1,2,0:T(8,128)(2,1)S(1)}, bf16[4,128,384]{1,2,0:T(8,128)(2,1)S(1)}, u32[]{:S(2)}, u32[]{:S(2)}) %collective-permute-start) | collective-permute-done | bytes 393248 | tf_op jit(solution)/shard_map/while/body/eval_jaxpr/ppermute | solution.py:12
  413.6 1.9 collective-permute-start
  415.8 12.6 %collective-permute-done = bf16[4,128,384]{1,2,0:T(8,128)(2,1)S(1)} collective-permute-done((bf16[4,128,384]{1,2,0:T(8,128)(2,1)S(1)}, bf16[4,128,384]{1,2,0:T(8,128)(2,1)S(1)}, u32[]{:S(2)}, u32[]{:S(2)}) %collective-permute-start) | collective-permute-done | bytes 393248 | tf_op jit(solution)/shard_map/while/body/eval_jaxpr/ppermute | solution.py:12
  432.4 13.7 %collective-permute-done = bf16[4,128,384]{1,2,0:T(8,128)(2,1)S(1)} collective-permute-done((bf16[4,128,384]{1,2,0:T(8,128)(2,1)S(1)}, bf16[4,128,384]{1,2,0:T(8,128)(2,1)S(1)}, u32[]{:S(2)}, u32[]{:S(2)}) %collective-permute-start) | collective-permute-done | bytes 393248 | tf_op jit(solution)/shard_map/while/body/eval_jaxpr/ppermute | solution.py:12
  450.0 13.6 %collective-permute-done = bf16[4,128,384]{1,2,0:T(8,128)(2,1)S(1)} collective-permute-done((bf16[4,128,384]{1,2,0:T(8,128)(2,1)S(1)}, bf16[4,128,384]{1,2,0:T(8,128)(2,1)S(1)}, u32[]{:S(2)}, u32[]{:S(2)}) %collective-permute-start) | collective-permute-done | bytes 393248 | tf_op jit(solution)/shard_map/while/body/eval_jaxpr/ppermute | solution.py:12
  465.3 1.9 collective-permute-start
  467.6 12.6 %collective-permute-done = bf16[4,128,384]{1,2,0:T(8,128)(2,1)S(1)} collective-permute-done((bf16[4,128,384]{1,2,0:T(8,128)(2,1)S(1)}, bf16[4,128,384]{1,2,0:T(8,128)(2,1)S(1)}, u32[]{:S(2)}, u32[]{:S(2)}) %collective-permute-start) | collective-permute-done | bytes 393248 | tf_op jit(solution)/shard_map/while/body/eval_jaxpr/ppermute | solution.py:12
  481.9 1.9 collective-permute-start
  484.2 11.7 %collective-permute-done = bf16[4,128,384]{1,2,0:T(8,128)(2,1)S(1)} collective-permute-done((bf16[4,128,384]{1,2,0:T(8,128)(2,1)S(1)}, bf16[4,128,384]{1,2,0:T(8,128)(2,1)S(1)}, u32[]{:S(2)}, u32[]{:S(2)}) %collective-permute-start) | collective-permute-done | bytes 393248 | tf_op jit(solution)/shard_map/while/body/eval_jaxpr/ppermute | solution.py:12
  498.2 3.6 convolution_convert_fusion
  501.8 4.7 copy.161
  506.5 3.6 copy.167
  510.1 91.5 %reduce-scatter.4.cloned.1.call-done = bf16[640,256]{1,0:T(8,128)(2,1)} async-done(((bf16[5120,256]{1,0:T(8,128)(2,1)}), bf16[640,256]{1,0:T(8,128)(2,1)}) %reduce-scatter.4.cloned.1.call-update) | async-done | bytes 327696
  (601 shorter events, 79.0 us)
Async XLA Ops:
  7.2 9.9 %copy-start = (s32[64]{0:T(128)S(1)}, s32[64]{0:T(128)}, u32[]{:S(2)}) copy-start(s32[64]{0:T(128)} %param.19) | copy-start | bytes 772
  7.2 594.5 %reduce-scatter.4.cloned.1.call-start = ((), (), s32[]{:S(2)}) async-start(), calls=%async_computation.1 | async-start | bytes 2949120
  17.1 23.2 %collective-permute-start = (bf16[4,128,384]{1,2,0:T(8,128)(2,1)S(1)}, bf16[4,128,384]{1,2,0:T(8,128)(2,1)S(1)}, u32[]{:S(2)}, u32[]{:S(2)}) collective-permute-start(bf16[4,128,384]{1,2,0:T(8,128)(2,1)S(1)} %get-tuple-element.578), channel_id=1, source_target_pairs={{0,16},{16,32},{32,48},{48,64},{64,80},{80,96},{96,112},{112,128},... | collective-permute-start | bytes 1179656 | tf_op jit(solution)/shard_map/while/body/eval_jaxpr/ppermute | solution.py:12
  42.0 14.9 %collective-permute-start = (bf16[4,128,384]{1,2,0:T(8,128)(2,1)S(1)}, bf16[4,128,384]{1,2,0:T(8,128)(2,1)S(1)}, u32[]{:S(2)}, u32[]{:S(2)}) collective-permute-start(bf16[4,128,384]{1,2,0:T(8,128)(2,1)S(1)} %get-tuple-element.578), channel_id=1, source_target_pairs={{0,16},{16,32},{32,48},{48,64},{64,80},{80,96},{96,112},{112,128},... | collective-permute-start | bytes 1179656 | tf_op jit(solution)/shard_map/while/body/eval_jaxpr/ppermute | solution.py:12
  58.6 14.0 %collective-permute-start = (bf16[4,128,384]{1,2,0:T(8,128)(2,1)S(1)}, bf16[4,128,384]{1,2,0:T(8,128)(2,1)S(1)}, u32[]{:S(2)}, u32[]{:S(2)}) collective-permute-start(bf16[4,128,384]{1,2,0:T(8,128)(2,1)S(1)} %get-tuple-element.578), channel_id=1, source_target_pairs={{0,16},{16,32},{32,48},{48,64},{64,80},{80,96},{96,112},{112,128},... | collective-permute-start | bytes 1179656 | tf_op jit(solution)/shard_map/while/body/eval_jaxpr/ppermute | solution.py:12
  74.3 13.0 %collective-permute-start = (bf16[4,128,384]{1,2,0:T(8,128)(2,1)S(1)}, bf16[4,128,384]{1,2,0:T(8,128)(2,1)S(1)}, u32[]{:S(2)}, u32[]{:S(2)}) collective-permute-start(bf16[4,128,384]{1,2,0:T(8,128)(2,1)S(1)} %get-tuple-element.578), channel_id=1, source_target_pairs={{0,16},{16,32},{32,48},{48,64},{64,80},{80,96},{96,112},{112,128},... | collective-permute-start | bytes 1179656 | tf_op jit(solution)/shard_map/while/body/eval_jaxpr/ppermute | solution.py:12
  89.0 12.1 %collective-permute-start = (bf16[4,128,384]{1,2,0:T(8,128)(2,1)S(1)}, bf16[4,128,384]{1,2,0:T(8,128)(2,1)S(1)}, u32[]{:S(2)}, u32[]{:S(2)}) collective-permute-start(bf16[4,128,384]{1,2,0:T(8,128)(2,1)S(1)} %get-tuple-element.578), channel_id=1, source_target_pairs={{0,16},{16,32},{32,48},{48,64},{64,80},{80,96},{96,112},{112,128},... | collective-permute-start | bytes 1179656 | tf_op jit(solution)/shard_map/while/body/eval_jaxpr/ppermute | solution.py:12
  102.8 12.1 %collective-permute-start = (bf16[4,128,384]{1,2,0:T(8,128)(2,1)S(1)}, bf16[4,128,384]{1,2,0:T(8,128)(2,1)S(1)}, u32[]{:S(2)}, u32[]{:S(2)}) collective-permute-start(bf16[4,128,384]{1,2,0:T(8,128)(2,1)S(1)} %get-tuple-element.578), channel_id=1, source_target_pairs={{0,16},{16,32},{32,48},{48,64},{64,80},{80,96},{96,112},{112,128},... | collective-permute-start | bytes 1179656 | tf_op jit(solution)/shard_map/while/body/eval_jaxpr/ppermute | solution.py:12
  116.7 12.1 %collective-permute-start = (bf16[4,128,384]{1,2,0:T(8,128)(2,1)S(1)}, bf16[4,128,384]{1,2,0:T(8,128)(2,1)S(1)}, u32[]{:S(2)}, u32[]{:S(2)}) collective-permute-start(bf16[4,128,384]{1,2,0:T(8,128)(2,1)S(1)} %get-tuple-element.578), channel_id=1, source_target_pairs={{0,16},{16,32},{32,48},{48,64},{64,80},{80,96},{96,112},{112,128},... | collective-permute-start | bytes 1179656 | tf_op jit(solution)/shard_map/while/body/eval_jaxpr/ppermute | solution.py:12
  130.5 12.1 %collective-permute-start = (bf16[4,128,384]{1,2,0:T(8,128)(2,1)S(1)}, bf16[4,128,384]{1,2,0:T(8,128)(2,1)S(1)}, u32[]{:S(2)}, u32[]{:S(2)}) collective-permute-start(bf16[4,128,384]{1,2,0:T(8,128)(2,1)S(1)} %get-tuple-element.578), channel_id=1, source_target_pairs={{0,16},{16,32},{32,48},{48,64},{64,80},{80,96},{96,112},{112,128},... | collective-permute-start | bytes 1179656 | tf_op jit(solution)/shard_map/while/body/eval_jaxpr/ppermute | solution.py:12
  144.3 12.1 %collective-permute-start = (bf16[4,128,384]{1,2,0:T(8,128)(2,1)S(1)}, bf16[4,128,384]{1,2,0:T(8,128)(2,1)S(1)}, u32[]{:S(2)}, u32[]{:S(2)}) collective-permute-start(bf16[4,128,384]{1,2,0:T(8,128)(2,1)S(1)} %get-tuple-element.578), channel_id=1, source_target_pairs={{0,16},{16,32},{32,48},{48,64},{64,80},{80,96},{96,112},{112,128},... | collective-permute-start | bytes 1179656 | tf_op jit(solution)/shard_map/while/body/eval_jaxpr/ppermute | solution.py:12
  158.2 12.1 %collective-permute-start = (bf16[4,128,384]{1,2,0:T(8,128)(2,1)S(1)}, bf16[4,128,384]{1,2,0:T(8,128)(2,1)S(1)}, u32[]{:S(2)}, u32[]{:S(2)}) collective-permute-start(bf16[4,128,384]{1,2,0:T(8,128)(2,1)S(1)} %get-tuple-element.578), channel_id=1, source_target_pairs={{0,16},{16,32},{32,48},{48,64},{64,80},{80,96},{96,112},{112,128},... | collective-permute-start | bytes 1179656 | tf_op jit(solution)/shard_map/while/body/eval_jaxpr/ppermute | solution.py:12
  172.0 12.7 %collective-permute-start = (bf16[4,128,384]{1,2,0:T(8,128)(2,1)S(1)}, bf16[4,128,384]{1,2,0:T(8,128)(2,1)S(1)}, u32[]{:S(2)}, u32[]{:S(2)}) collective-permute-start(bf16[4,128,384]{1,2,0:T(8,128)(2,1)S(1)} %get-tuple-element.578), channel_id=1, source_target_pairs={{0,16},{16,32},{32,48},{48,64},{64,80},{80,96},{96,112},{112,128},... | collective-permute-start | bytes 1179656 | tf_op jit(solution)/shard_map/while/body/eval_jaxpr/ppermute | solution.py:12
  186.4 13.8 %collective-permute-start = (bf16[4,128,384]{1,2,0:T(8,128)(2,1)S(1)}, bf16[4,128,384]{1,2,0:T(8,128)(2,1)S(1)}, u32[]{:S(2)}, u32[]{:S(2)}) collective-permute-start(bf16[4,128,384]{1,2,0:T(8,128)(2,1)S(1)} %get-tuple-element.578), channel_id=1, source_target_pairs={{0,16},{16,32},{32,48},{48,64},{64,80},{80,96},{96,112},{112,128},... | collective-permute-start | bytes 1179656 | tf_op jit(solution)/shard_map/while/body/eval_jaxpr/ppermute | solution.py:12
  201.9 14.9 %collective-permute-start = (bf16[4,128,384]{1,2,0:T(8,128)(2,1)S(1)}, bf16[4,128,384]{1,2,0:T(8,128)(2,1)S(1)}, u32[]{:S(2)}, u32[]{:S(2)}) collective-permute-start(bf16[4,128,384]{1,2,0:T(8,128)(2,1)S(1)} %get-tuple-element.578), channel_id=1, source_target_pairs={{0,16},{16,32},{32,48},{48,64},{64,80},{80,96},{96,112},{112,128},... | collective-permute-start | bytes 1179656 | tf_op jit(solution)/shard_map/while/body/eval_jaxpr/ppermute | solution.py:12
  218.5 16.0 %collective-permute-start = (bf16[4,128,384]{1,2,0:T(8,128)(2,1)S(1)}, bf16[4,128,384]{1,2,0:T(8,128)(2,1)S(1)}, u32[]{:S(2)}, u32[]{:S(2)}) collective-permute-start(bf16[4,128,384]{1,2,0:T(8,128)(2,1)S(1)} %get-tuple-element.578), channel_id=1, source_target_pairs={{0,16},{16,32},{32,48},{48,64},{64,80},{80,96},{96,112},{112,128},... | collective-permute-start | bytes 1179656 | tf_op jit(solution)/shard_map/while/body/eval_jaxpr/ppermute | solution.py:12
  236.1 15.8 %collective-permute-start = (bf16[4,128,384]{1,2,0:T(8,128)(2,1)S(1)}, bf16[4,128,384]{1,2,0:T(8,128)(2,1)S(1)}, u32[]{:S(2)}, u32[]{:S(2)}) collective-permute-start(bf16[4,128,384]{1,2,0:T(8,128)(2,1)S(1)} %get-tuple-element.578), channel_id=1, source_target_pairs={{0,16},{16,32},{32,48},{48,64},{64,80},{80,96},{96,112},{112,128},... | collective-permute-start | bytes 1179656 | tf_op jit(solution)/shard_map/while/body/eval_jaxpr/ppermute | solution.py:12
  253.7 14.9 %collective-permute-start = (bf16[4,128,384]{1,2,0:T(8,128)(2,1)S(1)}, bf16[4,128,384]{1,2,0:T(8,128)(2,1)S(1)}, u32[]{:S(2)}, u32[]{:S(2)}) collective-permute-start(bf16[4,128,384]{1,2,0:T(8,128)(2,1)S(1)} %get-tuple-element.578), channel_id=1, source_target_pairs={{0,16},{16,32},{32,48},{48,64},{64,80},{80,96},{96,112},{112,128},... | collective-permute-start | bytes 1179656 | tf_op jit(solution)/shard_map/while/body/eval_jaxpr/ppermute | solution.py:12
  270.3 14.0 %collective-permute-start = (bf16[4,128,384]{1,2,0:T(8,128)(2,1)S(1)}, bf16[4,128,384]{1,2,0:T(8,128)(2,1)S(1)}, u32[]{:S(2)}, u32[]{:S(2)}) collective-permute-start(bf16[4,128,384]{1,2,0:T(8,128)(2,1)S(1)} %get-tuple-element.578), channel_id=1, source_target_pairs={{0,16},{16,32},{32,48},{48,64},{64,80},{80,96},{96,112},{112,128},... | collective-permute-start | bytes 1179656 | tf_op jit(solution)/shard_map/while/body/eval_jaxpr/ppermute | solution.py:12
  285.9 13.0 %collective-permute-start = (bf16[4,128,384]{1,2,0:T(8,128)(2,1)S(1)}, bf16[4,128,384]{1,2,0:T(8,128)(2,1)S(1)}, u32[]{:S(2)}, u32[]{:S(2)}) collective-permute-start(bf16[4,128,384]{1,2,0:T(8,128)(2,1)S(1)} %get-tuple-element.578), channel_id=1, source_target_pairs={{0,16},{16,32},{32,48},{48,64},{64,80},{80,96},{96,112},{112,128},... | collective-permute-start | bytes 1179656 | tf_op jit(solution)/shard_map/while/body/eval_jaxpr/ppermute | solution.py:12
  300.7 12.1 %collective-permute-start = (bf16[4,128,384]{1,2,0:T(8,128)(2,1)S(1)}, bf16[4,128,384]{1,2,0:T(8,128)(2,1)S(1)}, u32[]{:S(2)}, u32[]{:S(2)}) collective-permute-start(bf16[4,128,384]{1,2,0:T(8,128)(2,1)S(1)} %get-tuple-element.578), channel_id=1, source_target_pairs={{0,16},{16,32},{32,48},{48,64},{64,80},{80,96},{96,112},{112,128},... | collective-permute-start | bytes 1179656 | tf_op jit(solution)/shard_map/while/body/eval_jaxpr/ppermute | solution.py:12
  314.5 12.1 %collective-permute-start = (bf16[4,128,384]{1,2,0:T(8,128)(2,1)S(1)}, bf16[4,128,384]{1,2,0:T(8,128)(2,1)S(1)}, u32[]{:S(2)}, u32[]{:S(2)}) collective-permute-start(bf16[4,128,384]{1,2,0:T(8,128)(2,1)S(1)} %get-tuple-element.578), channel_id=1, source_target_pairs={{0,16},{16,32},{32,48},{48,64},{64,80},{80,96},{96,112},{112,128},... | collective-permute-start | bytes 1179656 | tf_op jit(solution)/shard_map/while/body/eval_jaxpr/ppermute | solution.py:12
  328.3 12.1 %collective-permute-start = (bf16[4,128,384]{1,2,0:T(8,128)(2,1)S(1)}, bf16[4,128,384]{1,2,0:T(8,128)(2,1)S(1)}, u32[]{:S(2)}, u32[]{:S(2)}) collective-permute-start(bf16[4,128,384]{1,2,0:T(8,128)(2,1)S(1)} %get-tuple-element.578), channel_id=1, source_target_pairs={{0,16},{16,32},{32,48},{48,64},{64,80},{80,96},{96,112},{112,128},... | collective-permute-start | bytes 1179656 | tf_op jit(solution)/shard_map/while/body/eval_jaxpr/ppermute | solution.py:12
  342.2 12.1 %collective-permute-start = (bf16[4,128,384]{1,2,0:T(8,128)(2,1)S(1)}, bf16[4,128,384]{1,2,0:T(8,128)(2,1)S(1)}, u32[]{:S(2)}, u32[]{:S(2)}) collective-permute-start(bf16[4,128,384]{1,2,0:T(8,128)(2,1)S(1)} %get-tuple-element.578), channel_id=1, source_target_pairs={{0,16},{16,32},{32,48},{48,64},{64,80},{80,96},{96,112},{112,128},... | collective-permute-start | bytes 1179656 | tf_op jit(solution)/shard_map/while/body/eval_jaxpr/ppermute | solution.py:12
  356.0 12.1 %collective-permute-start = (bf16[4,128,384]{1,2,0:T(8,128)(2,1)S(1)}, bf16[4,128,384]{1,2,0:T(8,128)(2,1)S(1)}, u32[]{:S(2)}, u32[]{:S(2)}) collective-permute-start(bf16[4,128,384]{1,2,0:T(8,128)(2,1)S(1)} %get-tuple-element.578), channel_id=1, source_target_pairs={{0,16},{16,32},{32,48},{48,64},{64,80},{80,96},{96,112},{112,128},... | collective-permute-start | bytes 1179656 | tf_op jit(solution)/shard_map/while/body/eval_jaxpr/ppermute | solution.py:12
  369.8 12.1 %collective-permute-start = (bf16[4,128,384]{1,2,0:T(8,128)(2,1)S(1)}, bf16[4,128,384]{1,2,0:T(8,128)(2,1)S(1)}, u32[]{:S(2)}, u32[]{:S(2)}) collective-permute-start(bf16[4,128,384]{1,2,0:T(8,128)(2,1)S(1)} %get-tuple-element.578), channel_id=1, source_target_pairs={{0,16},{16,32},{32,48},{48,64},{64,80},{80,96},{96,112},{112,128},... | collective-permute-start | bytes 1179656 | tf_op jit(solution)/shard_map/while/body/eval_jaxpr/ppermute | solution.py:12
  383.7 12.7 %collective-permute-start = (bf16[4,128,384]{1,2,0:T(8,128)(2,1)S(1)}, bf16[4,128,384]{1,2,0:T(8,128)(2,1)S(1)}, u32[]{:S(2)}, u32[]{:S(2)}) collective-permute-start(bf16[4,128,384]{1,2,0:T(8,128)(2,1)S(1)} %get-tuple-element.578), channel_id=1, source_target_pairs={{0,16},{16,32},{32,48},{48,64},{64,80},{80,96},{96,112},{112,128},... | collective-permute-start | bytes 1179656 | tf_op jit(solution)/shard_map/while/body/eval_jaxpr/ppermute | solution.py:12
  398.1 13.8 %collective-permute-start = (bf16[4,128,384]{1,2,0:T(8,128)(2,1)S(1)}, bf16[4,128,384]{1,2,0:T(8,128)(2,1)S(1)}, u32[]{:S(2)}, u32[]{:S(2)}) collective-permute-start(bf16[4,128,384]{1,2,0:T(8,128)(2,1)S(1)} %get-tuple-element.578), channel_id=1, source_target_pairs={{0,16},{16,32},{32,48},{48,64},{64,80},{80,96},{96,112},{112,128},... | collective-permute-start | bytes 1179656 | tf_op jit(solution)/shard_map/while/body/eval_jaxpr/ppermute | solution.py:12
  413.6 14.9 %collective-permute-start = (bf16[4,128,384]{1,2,0:T(8,128)(2,1)S(1)}, bf16[4,128,384]{1,2,0:T(8,128)(2,1)S(1)}, u32[]{:S(2)}, u32[]{:S(2)}) collective-permute-start(bf16[4,128,384]{1,2,0:T(8,128)(2,1)S(1)} %get-tuple-element.578), channel_id=1, source_target_pairs={{0,16},{16,32},{32,48},{48,64},{64,80},{80,96},{96,112},{112,128},... | collective-permute-start | bytes 1179656 | tf_op jit(solution)/shard_map/while/body/eval_jaxpr/ppermute | solution.py:12
  430.1 16.0 %collective-permute-start = (bf16[4,128,384]{1,2,0:T(8,128)(2,1)S(1)}, bf16[4,128,384]{1,2,0:T(8,128)(2,1)S(1)}, u32[]{:S(2)}, u32[]{:S(2)}) collective-permute-start(bf16[4,128,384]{1,2,0:T(8,128)(2,1)S(1)} %get-tuple-element.578), channel_id=1, source_target_pairs={{0,16},{16,32},{32,48},{48,64},{64,80},{80,96},{96,112},{112,128},... | collective-permute-start | bytes 1179656 | tf_op jit(solution)/shard_map/while/body/eval_jaxpr/ppermute | solution.py:12
  447.8 15.8 %collective-permute-start = (bf16[4,128,384]{1,2,0:T(8,128)(2,1)S(1)}, bf16[4,128,384]{1,2,0:T(8,128)(2,1)S(1)}, u32[]{:S(2)}, u32[]{:S(2)}) collective-permute-start(bf16[4,128,384]{1,2,0:T(8,128)(2,1)S(1)} %get-tuple-element.578), channel_id=1, source_target_pairs={{0,16},{16,32},{32,48},{48,64},{64,80},{80,96},{96,112},{112,128},... | collective-permute-start | bytes 1179656 | tf_op jit(solution)/shard_map/while/body/eval_jaxpr/ppermute | solution.py:12
  465.3 14.9 %collective-permute-start = (bf16[4,128,384]{1,2,0:T(8,128)(2,1)S(1)}, bf16[4,128,384]{1,2,0:T(8,128)(2,1)S(1)}, u32[]{:S(2)}, u32[]{:S(2)}) collective-permute-start(bf16[4,128,384]{1,2,0:T(8,128)(2,1)S(1)} %get-tuple-element.578), channel_id=1, source_target_pairs={{0,16},{16,32},{32,48},{48,64},{64,80},{80,96},{96,112},{112,128},... | collective-permute-start | bytes 1179656 | tf_op jit(solution)/shard_map/while/body/eval_jaxpr/ppermute | solution.py:12
  481.9 14.0 %collective-permute-start = (bf16[4,128,384]{1,2,0:T(8,128)(2,1)S(1)}, bf16[4,128,384]{1,2,0:T(8,128)(2,1)S(1)}, u32[]{:S(2)}, u32[]{:S(2)}) collective-permute-start(bf16[4,128,384]{1,2,0:T(8,128)(2,1)S(1)} %get-tuple-element.578), channel_id=1, source_target_pairs={{0,16},{16,32},{32,48},{48,64},{64,80},{80,96},{96,112},{112,128},... | collective-permute-start | bytes 1179656 | tf_op jit(solution)/shard_map/while/body/eval_jaxpr/ppermute | solution.py:12
Sparse Core Ops, SparseCore 0:
  510.2 91.3 reduce-scatter.3
where the time goes:
time: 613 us; the launch traced here: 612 us
  waiting for transfers between devices  447 us (73%)
  starting transfers between devices  62 us (10%)
  matrix products  51.1 us (8%)
  local copies, waits for them, and re-layouts  20.7 us (3%)
  between operations  14.2 us (2%)
  other arithmetic  13.3 us (2%)
    ppermute x31, waiting for transfers between devices, shifted(): return lax.ppermute(value, axis, pairs)  355 us
    unnamed x2, waiting for transfers between devices  91.5 us
    ppermute x31, starting transfers between devices, shifted(): return lax.ppermute(value, axis, pairs)  62 us
    unnamed x13, local copies, waits for them, and re-layouts  17.1 us
  transfers between devices with their start and end apart: 32, of which 32 were waited for; matrix products, arithmetic and copies ran while one was open for 1% of the time, Pallas kernels for 0%

commit v1 on v0

v1 whole, which is shorter than its diff:
```python
import functools

import jax
import jax.numpy as jnp
from jax import lax
from jax.experimental import pallas as pl
from jax.experimental.pallas import tpu as pltpu
from jax.sharding import PartitionSpec as P

HDIM = 128
PIECES = 4
NONE_SEEN = -1e29
MASKED = -1e30


def dot(a, b):
    return lax.dot_general(a, b, (((1,), (0,)), ((), ())), preferred_element_type=jnp.float32)


def dot_nt(a, b):
    return lax.dot_general(a, b, (((1,), (1,)), ((), ())), preferred_element_type=jnp.float32)


def kernel(
    nz,
    n_head,
    q_in,
    k_in,
    v_in,
    tq_in,
    tk_in,
    tv_in,
    w_in,
    lengths,
    order,
    out,
    tan_out,
    stage,
    qbuf,
    kbuf,
    vbuf,
    wbuf,
    bounds,
    stats,
    acc,
    own_o,
    own_stats,
    o_send,
    s_send,
    o_recv,
    s_recv,
    gbuf,
    total,
    stage_sem,
    ring_send,
    ring_recv,
    q_sem,
    w_sem,
    w_own_sem,
    o_sem,
    s_sem,
    g_send,
    g_recv,
):
    rows = q_in.shape[0]
    heads = q_in.shape[1] // HDIM
    half = rows // 2
    clips = lengths.shape[0]
    depth = nz // 2
    ncol = wbuf.shape[2]
    scale = 1.0 / HDIM**0.5

    ctx = lax.axis_index("ctx")
    hd = lax.axis_index("head")
    column = ctx // nz
    z = ctx % nz
    right = column * nz + (z + 1) % nz
    left = column * nz + (z + nz - 1) % nz
    partner = (ctx + nz) % (2 * nz)

    stages = [
        pltpu.make_async_copy(ref, stage.at[i], stage_sem.at[i])
        for i, ref in enumerate((k_in, tk_in, v_in, tv_in, q_in, tq_in))
    ]
    for copy in stages:
        copy.start()
    own_w = pltpu.make_async_copy(
        w_in.at[:, :, pl.ds(pl.multiple_of(hd * ncol, 128), ncol)],
        wbuf.at[:, pl.ds(pl.multiple_of(hd * HDIM, HDIM), HDIM), :],
        w_own_sem,
    )
    own_w.start()

    barrier = pltpu.get_barrier_semaphore()
    for other in (right, left, partner):
        pl.semaphore_signal(barrier, inc=1, device_id={"ctx": other})
    for i in range(1, n_head):
        pl.semaphore_signal(barrier, inc=1, device_id={"head": (hd + i) % n_head})

    ends = []
    running = jnp.int32(0)
    for c in range(clips):
        running = running + lengths[c]
        ends.append(running)
    lane = lax.broadcasted_iota(jnp.int32, (1, rows), 1)
    for slot, index in enumerate((ctx, partner)):
        anchor = jnp.where(
            lane < half,
            order[2 * index] * half + lane,
            order[2 * index + 1] * half + lane - half,
        )
        low = jnp.zeros_like(anchor)
        high = jnp.full_like(anchor, rows * nz * 2)
        for end in ends:
            low = jnp.where(end <= anchor, jnp.maximum(low, end), low)
            high = jnp.where(end > anchor, jnp.minimum(high, end), high)
        bounds[0:1, slot * rows : (slot + 1) * rows] = low
        bounds[1:2, slot * rows : (slot + 1) * rows] = high

    for copy in stages:
        copy.wait()
    for h in range(heads):
        cols = slice(h * HDIM, (h + 1) * HDIM)
        kbuf[h, z, :, 0:HDIM] = stage[0, :, cols]
        kbuf[h, z, :, HDIM : 2 * HDIM] = stage[1, :, cols]
        vbuf[h, z, 0:HDIM, :] = stage[2, :, cols].astype(jnp.float32).T.astype(jnp.bfloat16)
        vbuf[h, z, HDIM : 2 * HDIM, :] = stage[3, :, cols].astype(jnp.float32).T.astype(jnp.bfloat16)
        qbuf[0, h, :, HDIM : 2 * HDIM] = stage[4, :, cols]
        qbuf[0, h, :, 0:HDIM] = stage[5, :, cols]

    def ring_copy(h, hop, piece, side):
        source = (z + nz - hop) % nz if side == 0 else (z + hop) % nz
        step = h * depth + hop
        buf = kbuf if piece < 2 else vbuf
        size = buf.shape[2] // 2
        ref = buf.at[h, source, pl.ds((piece % 2) * size, size), :]
        return pltpu.make_async_remote_copy(
            src_ref=ref,
            dst_ref=ref,
            send_sem=ring_send.at[side, piece, step % 2],
            recv_sem=ring_recv.at[side, piece, step],
            device_id={"ctx": right if side == 0 else left},
        )

    def q_copy(h):
        return pltpu.make_async_remote_copy(
            src_ref=qbuf.at[0, h],
            dst_ref=qbuf.at[1, h],
            send_sem=q_sem.at[0, h],
            recv_sem=q_sem.at[1, h],
            device_id={"ctx": partner},
        )

    def w_copy(i):
        other = (hd + i) % n_head
        return pltpu.make_async_remote_copy(
            src_ref=w_in.at[:, :, pl.ds(pl.multiple_of(other * ncol, 128), ncol)],
            dst_ref=wbuf.at[:, pl.ds(pl.multiple_of(hd * HDIM, HDIM), HDIM), :],
            send_sem=w_sem.at[0, i - 1],
            recv_sem=w_sem.at[1, i - 1],
            device_id={"head": other},
        )

    def o_copies(h):
        return [
            pltpu.make_async_remote_copy(
                src_ref=src.at[h],
                dst_ref=dst.at[h],
                send_sem=sem.at[0, h],
                recv_sem=sem.at[1, h],
                device_id={"ctx": partner},
            )
            for src, dst, sem in ((s_send, s_recv, s_sem), (o_send, o_recv, o_sem))
        ]

    def g_copy(h, i):
        return pltpu.make_async_remote_copy(
            src_ref=gbuf.at[h, hd],
            dst_ref=gbuf.at[h, hd],
            send_sem=g_send.at[h, i - 1],
            recv_sem=g_recv.at[h, i - 1],
            device_id={"head": (hd + i) % n_head},
        )

    pl.semaphore_wait(barrier, 2 + n_head)
    for piece in range(PIECES):
        for side in range(2):
            ring_copy(0, 0, piece, side).start()
    for h in range(heads):
        q_copy(h).start()
    for i in range(1, n_head):
        w_copy(i).start()
    total[...] = jnp.zeros_like(total)
    s_send[...] = jnp.zeros_like(s_send)

    def allowed_keys(source):
        low, high = bounds[0:1, :], bounds[1:2, :]
        index = column * nz + source
        position = lax.broadcasted_iota(jnp.int32, (half, 2 * rows), 0)
        parts = []
        for part in range(2):
            first = order[2 * index + part] * half
            parts.append(jnp.logical_and(position >= low - first, position < high - first))
        return parts

    def attend(h, first, second):
        key = jnp.concatenate([kbuf[h, first], kbuf[h, second]], axis=0)
        query = jnp.concatenate([qbuf[0, h], qbuf[1, h]], axis=0)
        scores = dot_nt(key[:, :HDIM], query[:, HDIM:]) * scale
        tan_scores = dot_nt(key, query) * scale
        masks = allowed_keys(first) + allowed_keys(second)
        masked = jnp.concatenate(
            [
                jnp.where(mask, scores[i * half : (i + 1) * half], MASKED)
                for i, mask in enumerate(masks)
            ],
            axis=0,
        )
        peak = stats[0:1, :]
        new_peak = jnp.maximum(peak, jnp.max(masked, axis=0, keepdims=True))
        weights = jnp.exp(masked - new_peak)
        rescale = jnp.exp(peak - new_peak)
        products = weights * tan_scores
        stats[0:1, :] = new_peak
        stats[1:2, :] = rescale * stats[1:2, :] + jnp.sum(weights, axis=0, keepdims=True)
        stats[2:3, :] = rescale * stats[2:3, :] + jnp.sum(products, axis=0, keepdims=True)
        value = jnp.concatenate([vbuf[h, first], vbuf[h, second]], axis=1)
        weights_b = weights.astype(jnp.bfloat16)
        both = dot(value, weights_b)
        moved = dot(value[:HDIM], products.astype(jnp.bfloat16))
        acc[0:HDIM, :] = rescale * acc[0:HDIM, :] + both[:HDIM]
        acc[HDIM:, :] = rescale * acc[HDIM:, :] + both[HDIM:] + moved

    def finish(h):
        sums = stats[1:2, :]
        inverse = jnp.where(sums > 0.0, 1.0 / jnp.where(sums > 0.0, sums, 1.0), 0.0)
        mean = stats[2:3, :] * inverse
        primal = acc[0:HDIM, :] * inverse
        tangent = acc[HDIM:, :] * inverse - mean * primal
        own_o[h, 0:HDIM, :] = primal[:, :rows]
        own_o[h, HDIM:, :] = tangent[:, :rows]
        o_send[h, 0:HDIM, :] = primal[:, rows:].astype(jnp.bfloat16)
        o_send[h, HDIM:, :] = tangent[:, rows:].astype(jnp.bfloat16)
        for i, row in enumerate((stats[0:1, :], sums, mean)):
            own_stats[h, i : i + 1, :] = row[:, :rows]
            s_send[h, i : i + 1, :] = row[:, rows:]
        for copy in o_copies(h):
            copy.start()

    def merge(h):
        for copy in o_copies(h):
            copy.wait()
        peaks, sums, means = [], [], []
        for ref in (own_stats, s_recv):
            peaks.append(ref[h, 0:1, :])
            sums.append(ref[h, 1:2, :])
            means.append(ref[h, 2:3, :])
        peak = jnp.maximum(peaks[0], peaks[1])
        shares = [sums[i] * jnp.exp(peaks[i] - peak) for i in range(2)]
        inverse = 1.0 / (shares[0] + shares[1])
        shares = [share * inverse for share in shares]
        mean = shares[0] * means[0] + shares[1] * means[1]
        primals = [own_o[h, 0:HDIM, :], o_recv[h, 0:HDIM, :].astype(jnp.float32)]
        tangents = [own_o[h, HDIM:, :], o_recv[h, HDIM:, :].astype(jnp.float32)]
        primal = shares[0] * primals[0] + shares[1] * primals[1]
        tangent = sum(
            shares[i] * (tangents[i] + (means[i] - mean) * primals[i]) for i in range(2)
        )
        gbuf[h, hd, 0:rows, :] = primal.T.astype(jnp.bfloat16)
        gbuf[h, hd, rows:, :] = tangent.T.astype(jnp.bfloat16)
        for i in range(1, n_head):
            g_copy(h, i).start()

    def project(h):
        for i in range(1, n_head):
            g_copy(h, i).wait()
        features = jnp.concatenate([gbuf[h, g] for g in range(n_head)], axis=1)
        total[...] += dot(features, wbuf[h])

    def step(index, carry):
        h = index // depth
        d = index % depth + 1

        for piece in range(PIECES):
            for side in range(2):
                crosses = (piece < 2) == (side == 0)

                def take(piece=piece, side=side, crosses=crosses):
                    arrived = ring_copy(h, d - 1, piece, side)
                    arrived.wait_recv()

                    @pl.when(d < depth if crosses else d < depth - 1)
                    def _():
                        ring_copy(h, d, piece, side).start()

                    arrived.wait_send()

                if crosses:
                    take()
                else:
                    pl.when(d < depth)(take)

        @pl.when(jnp.logical_and(d == depth - 1, h < heads - 1))
        def _():
            for piece in range(PIECES):
                for side in range(2):
                    ring_copy(h + 1, 0, piece, side).start()

        @pl.when(d == 1)
        def _():
            stats[0:1, :] = jnp.full((1, 2 * rows), NONE_SEEN, jnp.float32)
            stats[1:3, :] = jnp.zeros((2, 2 * rows), jnp.float32)
            acc[...] = jnp.zeros_like(acc)
            q_copy(h).wait()

        attend(h, (z + nz - d) % nz, (z + d % depth) % nz)

        @pl.when(jnp.logical_and(d == 2, h >= 1))
        def _():
            merge(h - 1)

        @pl.when(jnp.logical_and(d == depth // 2, h == heads - 1))
        def _():
            own_w.wait()
            for i in range(1, n_head):
                w_copy(i).wait()

        for early in range(heads - 1):

            @pl.when(jnp.logical_and(d == depth // 2 + early, h == heads - 1))
            def _(early=early):
                project(early)

        @pl.when(d == depth)
        def _():
            finish(h)

        return carry

    lax.fori_loop(0, heads * depth, step, 0)
    merge(heads - 1)
    project(heads - 1)
    out[...] = total[0:rows, :].astype(out.dtype)
    tan_out[...] = total[rows:, :].astype(tan_out.dtype)


def local(
    queries,
    keys,
    values,
    tan_queries,
    tan_keys,
    tan_values,
    out_weight,
    clip_lengths,
    stretch_order,
):
    rows, width = queries.shape
    heads = width // HDIM
    n_head = lax.axis_size("head")
    nz = lax.axis_size("ctx") // 2
    depth = nz // 2
    ncol = out_weight.shape[1] // n_head
    bf16, f32 = jnp.bfloat16, jnp.float32
    weight = out_weight.reshape(heads, HDIM, out_weight.shape[1])
    dma = pltpu.SemaphoreType.DMA
    anywhere = pl.BlockSpec(memory_space=pl.ANY)
    in_smem = pl.BlockSpec(memory_space=pltpu.SMEM)
    in_vmem = pl.BlockSpec(memory_space=pltpu.VMEM)
    return pl.pallas_call(
        functools.partial(kernel, nz, n_head),
        out_shape=(
            jax.ShapeDtypeStruct((rows, ncol), bf16),
            jax.ShapeDtypeStruct((rows, ncol), bf16),
        ),
        in_specs=[anywhere] * 7 + [in_smem] * 2,
        out_specs=(in_vmem, in_vmem),
        scratch_shapes=[
            pltpu.VMEM((6, rows, width), bf16),
            pltpu.VMEM((2, heads, rows, 2 * HDIM), bf16),
            pltpu.VMEM((heads, nz, rows, 2 * HDIM), bf16),
            pltpu.VMEM((heads, nz, 2 * HDIM, rows), bf16),
            pltpu.VMEM((heads, n_head * HDIM, ncol), bf16),
            pltpu.VMEM((8, 2 * rows), jnp.int32),
            pltpu.VMEM((8, 2 * rows), f32),
            pltpu.VMEM((2 * HDIM, 2 * rows), f32),
            pltpu.VMEM((heads, 2 * HDIM, rows), f32),
            pltpu.VMEM((heads, 8, rows), f32),
            pltpu.VMEM((heads, 2 * HDIM, rows), bf16),
            pltpu.VMEM((heads, 8, rows), f32),
            pltpu.VMEM((heads, 2 * HDIM, rows), bf16),
            pltpu.VMEM((heads, 8, rows), f32),
            pltpu.VMEM((heads, n_head, 2 * rows, HDIM), bf16),
            pltpu.VMEM((2 * rows, ncol), f32),
            dma((6,)),
            dma((2, PIECES, 2)),
            dma((2, PIECES, heads * depth)),
            dma((2, heads)),
            dma((2, n_head - 1)),
            dma,
            dma((2, heads)),
            dma((2, heads)),
            dma((heads, n_head - 1)),
            dma((heads, n_head - 1)),
        ],
        compiler_params=pltpu.CompilerParams(
            collective_id=0,
            has_side_effects=True,
            vmem_limit_bytes=40 * 1024 * 1024,
        ),
        cost_estimate=pl.CostEstimate(
            flops=2 * 6 * 2 * rows * nz * rows * width + 4 * rows * n_head * width * ncol,
            bytes_accessed=8 * 1024 * 1024,
            transcendentals=2 * rows * nz * rows * heads,
        ),
    )(
        queries,
        keys,
        values,
        tan_queries,
        tan_keys,
        tan_values,
        weight,
        clip_lengths,
        stretch_order,
    )


def solution(mesh):
    placed = P(("dp", "ctx"), "head")
    return jax.shard_map(
        local,
        mesh=mesh,
        in_specs=(placed,) * 6 + (P("head", None), P("dp"), P("dp")),
        out_specs=(placed, placed),
        check_vma=False,
    )
```

time: 613 us -> 135 us (0.22)
  the two profiles are of different devices: /device:TPU:1 before, /device:TPU:2 now
where the time goes in v1:
time: 135 us
  Pallas kernels  124 us (92%)
  local copies, waits for them, and re-layouts  10.1 us (7%)
    pallas_call x1, Pallas kernels, local(): pl.pallas_call(functools.partial(kernel, nz, n_head), out_shape=(jax.Shap...  124 us
    unnamed x20, local copies, waits for them, and re-layouts  10.1 us

profile of v1, /device:TPU:2, one launch (start us, length us, event | category | flops | bytes accessed | tf_op | source)
XLA Modules:
  0.0 135.0 jit_solution(6246657361091433031)
XLA Ops:
  0.6 0.0 copy-start
  0.6 2.1 %copy-done = bf16[384,5120]{1,0:T(8,128)(2,1)S(1)} copy-done((bf16[384,5120]{1,0:T(8,128)(2,1)S(1)}, bf16[384,5120]{1,0:T(8,128)(2,1)}, u32[]{:S(2)}) %copy-start) | copy-done | bytes 3932184
  2.7 0.0 copy-start.1
  2.7 0.9 copy-done.1
  3.6 0.0 copy-start.2
  3.6 0.9 copy-done.2
  4.5 0.0 copy-start.3
  4.5 0.9 copy-done.3
  5.4 0.0 copy-start.4
  5.4 0.9 copy-done.4
  6.3 0.0 copy-start.5
  6.3 0.9 copy-done.5
  7.2 0.0 copy-start.6
  7.2 0.9 copy-done.6
  8.1 0.0 copy-start.7
  8.1 0.7 copy-done.7
  8.8 0.0 copy-start.8
  8.8 0.7 copy-done.8
  9.4 124.3 %shard_map.104 = (bf16[128,640]{1,0:T(8,128)(2,1)S(1)}, bf16[128,640]{1,0:T(8,128)(2,1)S(1)}) custom-call(bf16[128,384]{1,0:T(8,128)(2,1)S(1)} %copy-done.1, bf16[128,384]{1,0:T(8,128)(2,1)S(1)} %copy-done.2, bf16[128,384]{1,0:T(8,128)(2,1)S(1)} %copy-done.3, bf16[128,384]{1,0:T(8,128)(2,1)S(1)} %copy-done.4, bf16[128,384]{1,0:T(8,128)(2,1)S(1)} %copy-done.5, ...), custom_call_target="tpu_custom_call" | custom-call | flops 3422552064 | bytes 8388608 | tf_op jit(solution)/shard_map/pallas_call | solution.py:370
  133.7 0.7 copy.13
  134.4 0.7 copy.14
Async XLA Ops:
  0.6 2.1 %copy-start = (bf16[384,5120]{1,0:T(8,128)(2,1)S(1)}, bf16[384,5120]{1,0:T(8,128)(2,1)}, u32[]{:S(2)}) copy-start(bf16[384,5120]{1,0:T(8,128)(2,1)} %param.15) | copy-start | bytes 11796484
  2.7 0.9 copy-start.1
  3.6 0.9 copy-start.2
  4.5 0.9 copy-start.3
  5.4 0.9 copy-start.4
  6.3 0.9 copy-start.5
  7.2 0.9 copy-start.6
  8.1 0.7 copy-start.7
  8.8 0.7 copy-start.8

commit v2 on v1

--- a/solution.py
+++ b/solution.py
@@ -43,6 +43,7 @@
     bounds,
     stats,
     acc,
+    factors,
     own_o,
     own_stats,
     o_send,
@@ -137,10 +138,15 @@
         return pltpu.make_async_remote_copy(
             src_ref=ref,
             dst_ref=ref,
-            send_sem=ring_send.at[side, piece, step % 2],
+            send_sem=ring_send.at[side, piece, h * 2 + hop % 2],
             recv_sem=ring_recv.at[side, piece, step],
             device_id={"ctx": right if side == 0 else left},
         )
+
+    def send_own(h):
+        for piece in range(PIECES):
+            for side in range(2):
+                ring_copy(h, 0, piece, side).start()
 
     def q_copy(h):
         return pltpu.make_async_remote_copy(
@@ -183,9 +189,8 @@
         )
 
     pl.semaphore_wait(barrier, 2 + n_head)
-    for piece in range(PIECES):
-        for side in range(2):
-            ring_copy(0, 0, piece, side).start()
+    for h in range(heads - 1):
+        send_own(h)
     for h in range(heads):
         q_copy(h).start()
     for i in range(1, n_head):
@@ -203,7 +208,7 @@
             parts.append(jnp.logical_and(position >= low - first, position < high - first))
         return parts
 
-    def attend(h, first, second):
+    def score(h, first, second):
         key = jnp.concatenate([kbuf[h, first], kbuf[h, second]], axis=0)
         query = jnp.concatenate([qbuf[0, h], qbuf[1, h]], axis=0)
         scores = dot_nt(key[:, :HDIM], query[:, HDIM:]) * scale
@@ -216,32 +221,37 @@
             ],
             axis=0,
         )
-        peak = stats[0:1, :]
+        peak = stats[h, 0:1, :]
         new_peak = jnp.maximum(peak, jnp.max(masked, axis=0, keepdims=True))
         weights = jnp.exp(masked - new_peak)
         rescale = jnp.exp(peak - new_peak)
         products = weights * tan_scores
-        stats[0:1, :] = new_peak
-        stats[1:2, :] = rescale * stats[1:2, :] + jnp.sum(weights, axis=0, keepdims=True)
-        stats[2:3, :] = rescale * stats[2:3, :] + jnp.sum(products, axis=0, keepdims=True)
+        stats[h, 0:1, :] = new_peak
+        stats[h, 1:2, :] = rescale * stats[h, 1:2, :] + jnp.sum(weights, axis=0, keepdims=True)
+        stats[h, 2:3, :] = rescale * stats[h, 2:3, :] + jnp.sum(products, axis=0, keepdims=True)
+        stats[h, 3:4, :] = rescale
+        factors[0] = weights.astype(jnp.bfloat16)
+        factors[1] = products.astype(jnp.bfloat16)
+
+    def apply(h, first, second):
         value = jnp.concatenate([vbuf[h, first], vbuf[h, second]], axis=1)
-        weights_b = weights.astype(jnp.bfloat16)
-        both = dot(value, weights_b)
-        moved = dot(value[:HDIM], products.astype(jnp.bfloat16))
-        acc[0:HDIM, :] = rescale * acc[0:HDIM, :] + both[:HDIM]
-        acc[HDIM:, :] = rescale * acc[HDIM:, :] + both[HDIM:] + moved
+        both = dot(value, factors[0])
+        moved = dot(value[:HDIM], factors[1])
+        rescale = stats[h, 3:4, :]
+        acc[h, 0:HDIM, :] = rescale * acc[h, 0:HDIM, :] + both[:HDIM]
+        acc[h, HDIM:, :] = rescale * acc[h, HDIM:, :] + both[HDIM:] + moved
 
     def finish(h):
-        sums = stats[1:2, :]
+        sums = stats[h, 1:2, :]
         inverse = jnp.where(sums > 0.0, 1.0 / jnp.where(sums > 0.0, sums, 1.0), 0.0)
-        mean = stats[2:3, :] * inverse
-        primal = acc[0:HDIM, :] * inverse
-        tangent = acc[HDIM:, :] * inverse - mean * primal
+        mean = stats[h, 2:3, :] * inverse
+        primal = acc[h, 0:HDIM, :] * inverse
+        tangent = acc[h, HDIM:, :] * inverse - mean * primal
         own_o[h, 0:HDIM, :] = primal[:, :rows]
         own_o[h, HDIM:, :] = tangent[:, :rows]
         o_send[h, 0:HDIM, :] = primal[:, rows:].astype(jnp.bfloat16)
         o_send[h, HDIM:, :] = tangent[:, rows:].astype(jnp.bfloat16)
-        for i, row in enumerate((stats[0:1, :], sums, mean)):
+        for i, row in enumerate((stats[h, 0:1, :], sums, mean)):
             own_stats[h, i : i + 1, :] = row[:, :rows]
             s_send[h, i : i + 1, :] = row[:, rows:]
         for copy in o_copies(h):
@@ -277,69 +287,90 @@
         features = jnp.concatenate([gbuf[h, g] for g in range(n_head)], axis=1)
         total[...] += dot(features, wbuf[h])
 
+    first_part = (heads - 1) * depth
+    steps = heads * depth
+
+    def place(index):
+        late = index // first_part
+        h = (1 - late) * (index % (heads - 1)) + late * (heads - 1)
+        d = (1 - late) * (index // (heads - 1)) + late * (index - first_part) + 1
+        return h, d
+
+    def forward(h, d, piece):
+        for side in range(2):
+            crosses = (piece < 2) == (side == 0)
+
+            def take(side=side, crosses=crosses):
+                arrived = ring_copy(h, d - 1, piece, side)
+                arrived.wait_recv()
+
+                @pl.when(d < depth if crosses else d < depth - 1)
+                def _():
+                    ring_copy(h, d, piece, side).start()
+
+                arrived.wait_send()
+
+            if crosses:
+                take()
+            else:
+                pl.when(d < depth)(take)
+
     def step(index, carry):
-        h = index // depth
-        d = index % depth + 1
-
-        for piece in range(PIECES):
-            for side in range(2):
-                crosses = (piece < 2) == (side == 0)
-
-                def take(piece=piece, side=side, crosses=crosses):
-                    arrived = ring_copy(h, d - 1, piece, side)
-                    arrived.wait_recv()
-
-                    @pl.when(d < depth if crosses else d < depth - 1)
-                    def _():
-                        ring_copy(h, d, piece, side).start()
-
-                    arrived.wait_send()
-
-                if crosses:
-                    take()
-                else:
-                    pl.when(d < depth)(take)
-
-        @pl.when(jnp.logical_and(d == depth - 1, h < heads - 1))
-        def _():
-            for piece in range(PIECES):
-                for side in range(2):
-                    ring_copy(h + 1, 0, piece, side).start()
-
-        @pl.when(d == 1)
-        def _():
-            stats[0:1, :] = jnp.full((1, 2 * rows), NONE_SEEN, jnp.float32)
-            stats[1:3, :] = jnp.zeros((2, 2 * rows), jnp.float32)
-            acc[...] = jnp.zeros_like(acc)
-            q_copy(h).wait()
-
-        attend(h, (z + nz - d) % nz, (z + d % depth) % nz)
-
-        @pl.when(jnp.logical_and(d == 2, h >= 1))
-        def _():
-            merge(h - 1)
-
-        @pl.when(jnp.logical_and(d == depth // 2, h == heads - 1))
-        def _():
-            own_w.wait()
-            for i in range(1, n_head):
-                w_copy(i).wait()
-
-        for early in range(heads - 1):
-
-            @pl.when(jnp.logical_and(d == depth // 2 + early, h == heads - 1))
-            def _(early=early):
-                project(early)
-
-        @pl.when(d == depth)
-        def _():
-            finish(h)
+        h, d = place(index)
+        old_h, old_d = place(jnp.maximum(index - 1, 0))
+        first, second = (z + nz - old_d) % nz, (z + old_d % depth) % nz
+        live = index < steps
+
+        @pl.when(live)
+        def _():
+            forward(h, d, 0)
+
+        @pl.when(index > 0)
+        def _():
+            @pl.when(old_d == 1)
+            def _():
+                stats[old_h, 0:1, :] = jnp.full((1, 2 * rows), NONE_SEEN, jnp.float32)
+                stats[old_h, 1:3, :] = jnp.zeros((2, 2 * rows), jnp.float32)
+                acc[old_h] = jnp.zeros((2 * HDIM, 2 * rows), jnp.float32)
+                q_copy(old_h).wait()
+
+            score(old_h, first, second)
+
+        @pl.when(live)
+        def _():
+            forward(h, d, 1)
+
+        @pl.when(index > 0)
+        def _():
+            apply(old_h, first, second)
+
+            @pl.when(old_d == depth)
+            def _():
+                finish(old_h)
+
+        @pl.when(live)
+        def _():
+            for piece in range(2, PIECES):
+                forward(h, d, piece)
+
+        @pl.when(jnp.logical_and(d == depth - 1, h == heads - 2))
+        def _():
+            send_own(heads - 1)
+
+        @pl.when(jnp.logical_and(index > first_part, index < first_part + heads))
+        def _():
+            merge(index - first_part - 1)
 
         return carry
 
-    lax.fori_loop(0, heads * depth, step, 0)
+    lax.fori_loop(0, steps + 1, step, 0)
+    own_w.wait()
+    for i in range(1, n_head):
+        w_copy(i).wait()
+    project(0)
     merge(heads - 1)
-    project(heads - 1)
+    for h in range(1, heads):
+        project(h)
     out[...] = total[0:rows, :].astype(out.dtype)
     tan_out[...] = total[rows:, :].astype(tan_out.dtype)
 
@@ -382,8 +413,9 @@
             pltpu.VMEM((heads, nz, 2 * HDIM, rows), bf16),
             pltpu.VMEM((heads, n_head * HDIM, ncol), bf16),
             pltpu.VMEM((8, 2 * rows), jnp.int32),
-            pltpu.VMEM((8, 2 * rows), f32),
-            pltpu.VMEM((2 * HDIM, 2 * rows), f32),
+            pltpu.VMEM((heads, 8, 2 * rows), f32),
+            pltpu.VMEM((heads, 2 * HDIM, 2 * rows), f32),
+            pltpu.VMEM((2, 2 * rows, 2 * rows), bf16),
             pltpu.VMEM((heads, 2 * HDIM, rows), f32),
             pltpu.VMEM((heads, 8, rows), f32),
             pltpu.VMEM((heads, 2 * HDIM, rows), bf16),
@@ -393,7 +425,7 @@
             pltpu.VMEM((heads, n_head, 2 * rows, HDIM), bf16),
             pltpu.VMEM((2 * rows, ncol), f32),
             dma((6,)),
-            dma((2, PIECES, 2)),
+            dma((2, PIECES, 2 * heads)),
             dma((2, PIECES, heads * depth)),
             dma((2, heads)),
             dma((2, n_head - 1)),
@@ -406,7 +438,7 @@
         compiler_params=pltpu.CompilerParams(
             collective_id=0,
             has_side_effects=True,
-            vmem_limit_bytes=40 * 1024 * 1024,
+            vmem_limit_bytes=60 * 1024 * 1024,
         ),
         cost_estimate=pl.CostEstimate(
             flops=2 * 6 * 2 * rows * nz * rows * width + 4 * rows * n_head * width * ncol,

time: 135 us -> 104 us (0.77)
  Pallas kernels: 124 us -> 99.9 us
  local copies, waits for them, and re-layouts: 10.1 us -> 3.19 us
    pallas_call x1, Pallas kernels: 124 us -> 99.9 us  [local(): pl.pallas_call(functools.partial(kernel, nz, n_head), out_shape=(jax.Shap...]
    unnamed x20 -> x2, local copies, waits for them, and re-layouts: 10.1 us -> 3.19 us
where the time goes in v2:
time: 104 us
  Pallas kernels  99.9 us (96%)
  local copies, waits for them, and re-layouts  3.19 us (3%)
    pallas_call x1, Pallas kernels, local(): pl.pallas_call(functools.partial(kernel, nz, n_head), out_shape=(jax.Shap...  99.9 us
    unnamed x2, local copies, waits for them, and re-layouts  3.19 us

profile of v2, /device:TPU:2, one launch (start us, length us, event | category | flops | bytes accessed | tf_op | source)
XLA Modules:
  0.0 103.7 jit_solution(727973645861133022)
XLA Ops:
  0.6 99.9 %shard_map.104 = (bf16[128,640]{1,0:T(8,128)(2,1)}, bf16[128,640]{1,0:T(8,128)(2,1)}) custom-call(bf16[128,384]{1,0:T(8,128)(2,1)} %q_in.1, bf16[128,384]{1,0:T(8,128)(2,1)} %k_in.1, bf16[128,384]{1,0:T(8,128)(2,1)} %v_in.1, bf16[128,384]{1,0:T(8,128)(2,1)} %tq_in.1, bf16[128,384]{1,0:T(8,128)(2,1)} %tk_in.1, bf16[128,384]{1,0:T(8,128)(2,1)} %tv_in.1, ...), custom_call_target="tpu_custom_call" | custom-call | flops 3422552064 | bytes 8388608 | tf_op jit(solution)/shard_map/pallas_call | solution.py:401
  100.5 1.6 %copy.13 = bf16[128,640]{1,0:T(8,128)(2,1)} copy(bf16[128,640]{1,0:T(8,128)(2,1)} %get-tuple-element.4) | data formatting | bytes 327680
  102.1 1.6 %copy.14 = bf16[128,640]{1,0:T(8,128)(2,1)} copy(bf16[128,640]{1,0:T(8,128)(2,1)} %get-tuple-element.5) | data formatting | bytes 327680

commit v3 on v2

--- a/solution.py
+++ b/solution.py
@@ -34,7 +34,6 @@
     lengths,
     order,
     out,
-    tan_out,
     stage,
     qbuf,
     kbuf,
@@ -157,13 +156,13 @@
             device_id={"ctx": partner},
         )
 
-    def w_copy(i):
+    def w_copy(h, i):
         other = (hd + i) % n_head
         return pltpu.make_async_remote_copy(
-            src_ref=w_in.at[:, :, pl.ds(pl.multiple_of(other * ncol, 128), ncol)],
-            dst_ref=wbuf.at[:, pl.ds(pl.multiple_of(hd * HDIM, HDIM), HDIM), :],
-            send_sem=w_sem.at[0, i - 1],
-            recv_sem=w_sem.at[1, i - 1],
+            src_ref=w_in.at[h, :, pl.ds(pl.multiple_of(other * ncol, 128), ncol)],
+            dst_ref=wbuf.at[h, pl.ds(pl.multiple_of(hd * HDIM, HDIM), HDIM), :],
+            send_sem=w_sem.at[0, h, i - 1],
+            recv_sem=w_sem.at[1, h, i - 1],
             device_id={"head": other},
         )
 
@@ -193,8 +192,6 @@
         send_own(h)
     for h in range(heads):
         q_copy(h).start()
-    for i in range(1, n_head):
-        w_copy(i).start()
     total[...] = jnp.zeros_like(total)
     s_send[...] = jnp.zeros_like(s_send)
 
@@ -283,6 +280,7 @@
 
     def project(h):
         for i in range(1, n_head):
+            w_copy(h, i).wait()
             g_copy(h, i).wait()
         features = jnp.concatenate([gbuf[h, g] for g in range(n_head)], axis=1)
         total[...] += dot(features, wbuf[h])
@@ -353,6 +351,10 @@
             for piece in range(2, PIECES):
                 forward(h, d, piece)
 
+        @pl.when(index < heads * (n_head - 1))
+        def _():
+            w_copy(index // (n_head - 1), index % (n_head - 1) + 1).start()
+
         @pl.when(jnp.logical_and(d == depth - 1, h == heads - 2))
         def _():
             send_own(heads - 1)
@@ -365,14 +367,11 @@
 
     lax.fori_loop(0, steps + 1, step, 0)
     own_w.wait()
-    for i in range(1, n_head):
-        w_copy(i).wait()
     project(0)
     merge(heads - 1)
     for h in range(1, heads):
         project(h)
-    out[...] = total[0:rows, :].astype(out.dtype)
-    tan_out[...] = total[rows:, :].astype(tan_out.dtype)
+    out[...] = total[...].astype(out.dtype)
 
 
 def local(
@@ -398,14 +397,11 @@
     anywhere = pl.BlockSpec(memory_space=pl.ANY)
     in_smem = pl.BlockSpec(memory_space=pltpu.SMEM)
     in_vmem = pl.BlockSpec(memory_space=pltpu.VMEM)
-    return pl.pallas_call(
+    both = pl.pallas_call(
         functools.partial(kernel, nz, n_head),
-        out_shape=(
-            jax.ShapeDtypeStruct((rows, ncol), bf16),
-            jax.ShapeDtypeStruct((rows, ncol), bf16),
-        ),
+        out_shape=jax.ShapeDtypeStruct((2 * rows, ncol), bf16),
         in_specs=[anywhere] * 7 + [in_smem] * 2,
-        out_specs=(in_vmem, in_vmem),
+        out_specs=in_vmem,
         scratch_shapes=[
             pltpu.VMEM((6, rows, width), bf16),
             pltpu.VMEM((2, heads, rows, 2 * HDIM), bf16),
@@ -428,7 +424,7 @@
             dma((2, PIECES, 2 * heads)),
             dma((2, PIECES, heads * depth)),
             dma((2, heads)),
-            dma((2, n_head - 1)),
+            dma((2, heads, n_head - 1)),
             dma,
             dma((2, heads)),
             dma((2, heads)),
@@ -456,6 +452,7 @@
         clip_lengths,
         stretch_order,
     )
+    return both[:rows], both[rows:]
 
 
 def solution(mesh):

time: 104 us -> 104 us (level)
  the two profiles are of different devices: /device:TPU:2 before, /device:TPU:32 now
where the time goes in v3:
time: 104 us
  Pallas kernels  102 us (98%)
  local copies, waits for them, and re-layouts  1.75 us (2%)
    pallas_call x1, Pallas kernels, local(): pl.pallas_call(functools.partial(kernel, nz, n_head), out_shape=jax.Shape...  102 us

profile of v3, /device:TPU:32, one launch (start us, length us, event | category | flops | bytes accessed | tf_op | source)
XLA Modules:
  0.0 103.9 jit_solution(13013480286660948770)
XLA Ops:
  0.6 101.6 %shard_map.104 = bf16[256,640]{1,0:T(8,128)(2,1)} custom-call(bf16[128,384]{1,0:T(8,128)(2,1)} %q_in.1, bf16[128,384]{1,0:T(8,128)(2,1)} %k_in.1, bf16[128,384]{1,0:T(8,128)(2,1)} %v_in.1, bf16[128,384]{1,0:T(8,128)(2,1)} %tq_in.1, bf16[128,384]{1,0:T(8,128)(2,1)} %tk_in.1, bf16[128,384]{1,0:T(8,128)(2,1)} %tv_in.1, bf16[3,128,5120]{2,1,0:T(8,128)(2,1)} %bitcast.1, ...), custom_call_target="tpu_custom_call" | custom-call | flops 3422552064 | bytes 8388608 | tf_op jit(solution)/shard_map/pallas_call | solution.py:400
  102.2 1.7 %fusion = (bf16[128,640]{1,0:T(8,128)(2,1)}, bf16[128,640]{1,0:T(8,128)(2,1)}) fusion(bf16[256,640]{1,0:T(8,128)(2,1)} %shard_map.104), kind=kLoop, calls=%fused_computation | loop fusion | bytes 655360 | tf_op jit(solution)/shard_map/slice | solution.py:455

commit v4 on v3

--- a/solution.py
+++ b/solution.py
@@ -68,10 +68,12 @@
     clips = lengths.shape[0]
     depth = nz // 2
     ncol = wbuf.shape[2]
+    w_half = HDIM // 2
     scale = 1.0 / HDIM**0.5
 
     ctx = lax.axis_index("ctx")
     hd = lax.axis_index("head")
+    core = lax.axis_index("dp")
     column = ctx // nz
     z = ctx % nz
     right = column * nz + (z + 1) % nz
@@ -96,6 +98,7 @@
         pl.semaphore_signal(barrier, inc=1, device_id={"ctx": other})
     for i in range(1, n_head):
         pl.semaphore_signal(barrier, inc=1, device_id={"head": (hd + i) % n_head})
+    pl.semaphore_signal(barrier, inc=1, device_id={"dp": 1 - core})
 
     ends = []
     running = jnp.int32(0)
@@ -116,17 +119,6 @@
             high = jnp.where(end > anchor, jnp.minimum(high, end), high)
         bounds[0:1, slot * rows : (slot + 1) * rows] = low
         bounds[1:2, slot * rows : (slot + 1) * rows] = high
-
-    for copy in stages:
-        copy.wait()
-    for h in range(heads):
-        cols = slice(h * HDIM, (h + 1) * HDIM)
-        kbuf[h, z, :, 0:HDIM] = stage[0, :, cols]
-        kbuf[h, z, :, HDIM : 2 * HDIM] = stage[1, :, cols]
-        vbuf[h, z, 0:HDIM, :] = stage[2, :, cols].astype(jnp.float32).T.astype(jnp.bfloat16)
-        vbuf[h, z, HDIM : 2 * HDIM, :] = stage[3, :, cols].astype(jnp.float32).T.astype(jnp.bfloat16)
-        qbuf[0, h, :, HDIM : 2 * HDIM] = stage[4, :, cols]
-        qbuf[0, h, :, 0:HDIM] = stage[5, :, cols]
 
     def ring_copy(h, hop, piece, side):
         source = (z + nz - hop) % nz if side == 0 else (z + hop) % nz
@@ -142,8 +134,8 @@
             device_id={"ctx": right if side == 0 else left},
         )
 
-    def send_own(h):
-        for piece in range(PIECES):
+    def send_own(h, pieces):
+        for piece in pieces:
             for side in range(2):
                 ring_copy(h, 0, piece, side).start()
 
@@ -156,14 +148,29 @@
             device_id={"ctx": partner},
         )
 
-    def w_copy(h, i):
+    def w_copy(i):
         other = (hd + i) % n_head
         return pltpu.make_async_remote_copy(
-            src_ref=w_in.at[h, :, pl.ds(pl.multiple_of(other * ncol, 128), ncol)],
-            dst_ref=wbuf.at[h, pl.ds(pl.multiple_of(hd * HDIM, HDIM), HDIM), :],
-            send_sem=w_sem.at[0, h, i - 1],
-            recv_sem=w_sem.at[1, h, i - 1],
+            src_ref=w_in.at[
+                :,
+                pl.ds(pl.multiple_of(core * w_half, w_half), w_half),
+                pl.ds(pl.multiple_of(other * ncol, 128), ncol),
+            ],
+            dst_ref=wbuf.at[:, pl.ds(pl.multiple_of(hd * HDIM + core * w_half, w_half), w_half), :],
+            send_sem=w_sem.at[0, i - 1],
+            recv_sem=w_sem.at[1, i - 1],
             device_id={"head": other},
+        )
+
+    def w_share(i):
+        source = (hd + n_head - i) % n_head
+        ref = wbuf.at[:, pl.ds(pl.multiple_of(source * HDIM + core * w_half, w_half), w_half), :]
+        return pltpu.make_async_remote_copy(
+            src_ref=ref,
+            dst_ref=ref,
+            send_sem=w_sem.at[2, i - 1],
+            recv_sem=w_sem.at[3, i - 1],
+            device_id={"dp": 1 - core},
         )
 
     def o_copies(h):
@@ -187,11 +194,30 @@
             device_id={"head": (hd + i) % n_head},
         )
 
-    pl.semaphore_wait(barrier, 2 + n_head)
-    for h in range(heads - 1):
-        send_own(h)
-    for h in range(heads):
+    columns = [slice(h * HDIM, (h + 1) * HDIM) for h in range(heads)]
+    for copy in stages[:2]:
+        copy.wait()
+    for h, cols in enumerate(columns):
+        kbuf[h, z, :, 0:HDIM] = stage[0, :, cols]
+        kbuf[h, z, :, HDIM : 2 * HDIM] = stage[1, :, cols]
+    pl.semaphore_wait(barrier, 3 + n_head)
+    send_own(0, range(2))
+    for copy in stages[2:4]:
+        copy.wait()
+    for h, cols in enumerate(columns):
+        vbuf[h, z, 0:HDIM, :] = stage[2, :, cols].astype(jnp.float32).T.astype(jnp.bfloat16)
+        vbuf[h, z, HDIM : 2 * HDIM, :] = stage[3, :, cols].astype(jnp.float32).T.astype(jnp.bfloat16)
+    send_own(0, range(2, PIECES))
+    for h in range(1, heads - 1):
+        send_own(h, range(PIECES))
+    for copy in stages[4:]:
+        copy.wait()
+    for h, cols in enumerate(columns):
+        qbuf[0, h, :, HDIM : 2 * HDIM] = stage[4, :, cols]
+        qbuf[0, h, :, 0:HDIM] = stage[5, :, cols]
         q_copy(h).start()
+    for i in range(1, n_head):
+        w_copy(i).start()
     total[...] = jnp.zeros_like(total)
     s_send[...] = jnp.zeros_like(s_send)
 
@@ -280,7 +306,6 @@
 
     def project(h):
         for i in range(1, n_head):
-            w_copy(h, i).wait()
             g_copy(h, i).wait()
         features = jnp.concatenate([gbuf[h, g] for g in range(n_head)], axis=1)
         total[...] += dot(features, wbuf[h])
@@ -351,13 +376,15 @@
             for piece in range(2, PIECES):
                 forward(h, d, piece)
 
-        @pl.when(index < heads * (n_head - 1))
-        def _():
-            w_copy(index // (n_head - 1), index % (n_head - 1) + 1).start()
+        @pl.when(index == first_part)
+        def _():
+            for i in range(1, n_head):
+                w_copy(i).wait()
+                w_share(i).start()
 
         @pl.when(jnp.logical_and(d == depth - 1, h == heads - 2))
         def _():
-            send_own(heads - 1)
+            send_own(heads - 1, range(PIECES))
 
         @pl.when(jnp.logical_and(index > first_part, index < first_part + heads))
         def _():
@@ -367,6 +394,8 @@
 
     lax.fori_loop(0, steps + 1, step, 0)
     own_w.wait()
+    for i in range(1, n_head):
+        w_share(i).wait()
     project(0)
     merge(heads - 1)
     for h in range(1, heads):
@@ -424,7 +453,7 @@
             dma((2, PIECES, 2 * heads)),
             dma((2, PIECES, heads * depth)),
             dma((2, heads)),
-            dma((2, heads, n_head - 1)),
+            dma((4, n_head - 1)),
             dma,
             dma((2, heads)),
             dma((2, heads)),

time: 104 us -> 102 us (0.981)
  the two profiles are of different devices: /device:TPU:32 before, /device:TPU:2 now
where the time goes in v4:
time: 102 us
  Pallas kernels  99.9 us (98%)
  local copies, waits for them, and re-layouts  1.75 us (2%)
    pallas_call x1, Pallas kernels, local(): pl.pallas_call(functools.partial(kernel, nz, n_head), out_shape=jax.Shape...  99.9 us

profile of v4, /device:TPU:2, one launch (start us, length us, event | category | flops | bytes accessed | tf_op | source)
XLA Modules:
  0.0 102.3 jit_solution(16580589331122645095)
XLA Ops:
  0.6 99.9 %shard_map.104 = bf16[256,640]{1,0:T(8,128)(2,1)} custom-call(bf16[128,384]{1,0:T(8,128)(2,1)} %q_in.1, bf16[128,384]{1,0:T(8,128)(2,1)} %k_in.1, bf16[128,384]{1,0:T(8,128)(2,1)} %v_in.1, bf16[128,384]{1,0:T(8,128)(2,1)} %tq_in.1, bf16[128,384]{1,0:T(8,128)(2,1)} %tk_in.1, bf16[128,384]{1,0:T(8,128)(2,1)} %tv_in.1, bf16[3,128,5120]{2,1,0:T(8,128)(2,1)} %bitcast.1, ...), custom_call_target="tpu_custom_call" | custom-call | flops 3422552064 | bytes 8388608 | tf_op jit(solution)/shard_map/pallas_call | solution.py:429
  100.6 1.7 %fusion = (bf16[128,640]{1,0:T(8,128)(2,1)}, bf16[128,640]{1,0:T(8,128)(2,1)}) fusion(bf16[256,640]{1,0:T(8,128)(2,1)} %shard_map.104), kind=kLoop, calls=%fused_computation | loop fusion | bytes 655360 | tf_op jit(solution)/shard_map/slice | solution.py:484

commit v5 on v4

--- a/solution.py
+++ b/solution.py
@@ -31,9 +31,11 @@
     tk_in,
     tv_in,
     w_in,
+    lengths_in,
+    order_in,
+    out,
     lengths,
     order,
-    out,
     stage,
     qbuf,
     kbuf,
@@ -84,7 +86,11 @@
         pltpu.make_async_copy(ref, stage.at[i], stage_sem.at[i])
         for i, ref in enumerate((k_in, tk_in, v_in, tv_in, q_in, tq_in))
     ]
-    for copy in stages:
+    tables = [
+        pltpu.make_async_copy(src, dst, stage_sem.at[6 + i])
+        for i, (src, dst) in enumerate(((lengths_in, lengths), (order_in, order)))
+    ]
+    for copy in stages + tables:
         copy.start()
     own_w = pltpu.make_async_copy(
         w_in.at[:, :, pl.ds(pl.multiple_of(hd * ncol, 128), ncol)],
@@ -100,6 +106,8 @@
         pl.semaphore_signal(barrier, inc=1, device_id={"head": (hd + i) % n_head})
     pl.semaphore_signal(barrier, inc=1, device_id={"dp": 1 - core})
 
+    for copy in tables:
+        copy.wait()
     ends = []
     running = jnp.int32(0)
     for c in range(clips):
@@ -310,13 +318,23 @@
         features = jnp.concatenate([gbuf[h, g] for g in range(n_head)], axis=1)
         total[...] += dot(features, wbuf[h])
 
-    first_part = (heads - 1) * depth
+    mid = 3 * depth // 2
+    late = mid + depth
     steps = heads * depth
 
     def place(index):
-        late = index // first_part
-        h = (1 - late) * (index % (heads - 1)) + late * (heads - 1)
-        d = (1 - late) * (index // (heads - 1)) + late * (index - first_part) + 1
+        group, turn = index // 3, index % 3
+        slow = turn % 2
+        h_a = slow
+        d_a = (1 - slow) * (2 * group + turn // 2 + 1) + slow * (group + 1)
+        pair, new = (index - mid) // 2, (index - mid) % 2
+        h_b = 1 + new
+        d_b = pair + 1 + (1 - new) * (depth // 2)
+        d_c = depth // 2 + index - late + 1
+        past_mid = jnp.minimum(index // mid, 1)
+        past_late = jnp.minimum(index // late, 1)
+        h = (1 - past_mid) * h_a + (past_mid - past_late) * h_b + past_late * 2
+        d = (1 - past_mid) * d_a + (past_mid - past_late) * d_b + past_late * d_c
         return h, d
 
     def forward(h, d, piece):
@@ -376,19 +394,21 @@
             for piece in range(2, PIECES):
                 forward(h, d, piece)
 
-        @pl.when(index == first_part)
+        @pl.when(index == late - 2)
         def _():
             for i in range(1, n_head):
                 w_copy(i).wait()
                 w_share(i).start()
 
-        @pl.when(jnp.logical_and(d == depth - 1, h == heads - 2))
+        @pl.when(jnp.logical_and(d == depth - 1, h == 0))
         def _():
             send_own(heads - 1, range(PIECES))
 
-        @pl.when(jnp.logical_and(index > first_part, index < first_part + heads))
-        def _():
-            merge(index - first_part - 1)
+        for early, when in ((0, mid + 2), (1, late + 1)):
+
+            @pl.when(index == when)
+            def _(early=early):
+                merge(early)
 
         return carry
 
@@ -424,14 +444,15 @@
     weight = out_weight.reshape(heads, HDIM, out_weight.shape[1])
     dma = pltpu.SemaphoreType.DMA
     anywhere = pl.BlockSpec(memory_space=pl.ANY)
-    in_smem = pl.BlockSpec(memory_space=pltpu.SMEM)
     in_vmem = pl.BlockSpec(memory_space=pltpu.VMEM)
     both = pl.pallas_call(
         functools.partial(kernel, nz, n_head),
         out_shape=jax.ShapeDtypeStruct((2 * rows, ncol), bf16),
-        in_specs=[anywhere] * 7 + [in_smem] * 2,
+        in_specs=[anywhere] * 9,
         out_specs=in_vmem,
         scratch_shapes=[
+            pltpu.SMEM(clip_lengths.shape, jnp.int32),
+            pltpu.SMEM(stretch_order.shape, jnp.int32),
             pltpu.VMEM((6, rows, width), bf16),
             pltpu.VMEM((2, heads, rows, 2 * HDIM), bf16),
             pltpu.VMEM((heads, nz, rows, 2 * HDIM), bf16),
@@ -449,7 +470,7 @@
             pltpu.VMEM((heads, 8, rows), f32),
             pltpu.VMEM((heads, n_head, 2 * rows, HDIM), bf16),
             pltpu.VMEM((2 * rows, ncol), f32),
-            dma((6,)),
+            dma((8,)),
             dma((2, PIECES, 2 * heads)),
             dma((2, PIECES, heads * depth)),
             dma((2, heads)),

time: 102 us -> 101 us (level)
  Pallas kernels: 99.9 us -> 98.5 us
    pallas_call x1, Pallas kernels: 99.9 us -> 98.5 us  [local(): pl.pallas_call(functools.partial(kernel, nz, n_head), out_shape=jax.Shape...]
where the time goes in v5:
time: 101 us
  Pallas kernels  98.5 us (98%)
  local copies, waits for them, and re-layouts  1.75 us (2%)
    pallas_call x1, Pallas kernels, local(): pl.pallas_call(functools.partial(kernel, nz, n_head), out_shape=jax.Shape...  98.5 us

profile of v5, /device:TPU:2, one launch (start us, length us, event | category | flops | bytes accessed | tf_op | source)
XLA Modules:
  0.0 100.9 jit_solution(17232332233997524339)
XLA Ops:
  0.6 98.5 %shard_map.104 = bf16[256,640]{1,0:T(8,128)(2,1)} custom-call(bf16[128,384]{1,0:T(8,128)(2,1)} %q_in.1, bf16[128,384]{1,0:T(8,128)(2,1)} %k_in.1, bf16[128,384]{1,0:T(8,128)(2,1)} %v_in.1, bf16[128,384]{1,0:T(8,128)(2,1)} %tq_in.1, bf16[128,384]{1,0:T(8,128)(2,1)} %tk_in.1, bf16[128,384]{1,0:T(8,128)(2,1)} %tv_in.1, bf16[3,128,5120]{2,1,0:T(8,128)(2,1)} %bitcast.1, ...), custom_call_target="tpu_custom_call" | custom-call | flops 3422552064 | bytes 8388608 | tf_op jit(solution)/shard_map/pallas_call | solution.py:448
  99.2 1.7 %fusion = (bf16[128,640]{1,0:T(8,128)(2,1)}, bf16[128,640]{1,0:T(8,128)(2,1)}) fusion(bf16[256,640]{1,0:T(8,128)(2,1)} %shard_map.104), kind=kLoop, calls=%fused_computation | loop fusion | bytes 655360 | tf_op jit(solution)/shard_map/slice | solution.py:505

commit v6 on v5

--- a/solution.py
+++ b/solution.py
@@ -8,7 +8,7 @@
 from jax.sharding import PartitionSpec as P
 
 HDIM = 128
-PIECES = 4
+PIECES = 2
 NONE_SEEN = -1e29
 MASKED = -1e30
 
@@ -131,9 +131,7 @@
     def ring_copy(h, hop, piece, side):
         source = (z + nz - hop) % nz if side == 0 else (z + hop) % nz
         step = h * depth + hop
-        buf = kbuf if piece < 2 else vbuf
-        size = buf.shape[2] // 2
-        ref = buf.at[h, source, pl.ds((piece % 2) * size, size), :]
+        ref = (kbuf, vbuf)[piece].at[h, source]
         return pltpu.make_async_remote_copy(
             src_ref=ref,
             dst_ref=ref,
@@ -209,13 +207,13 @@
         kbuf[h, z, :, 0:HDIM] = stage[0, :, cols]
         kbuf[h, z, :, HDIM : 2 * HDIM] = stage[1, :, cols]
     pl.semaphore_wait(barrier, 3 + n_head)
-    send_own(0, range(2))
+    send_own(0, [0])
     for copy in stages[2:4]:
         copy.wait()
     for h, cols in enumerate(columns):
         vbuf[h, z, 0:HDIM, :] = stage[2, :, cols].astype(jnp.float32).T.astype(jnp.bfloat16)
         vbuf[h, z, HDIM : 2 * HDIM, :] = stage[3, :, cols].astype(jnp.float32).T.astype(jnp.bfloat16)
-    send_own(0, range(2, PIECES))
+    send_own(0, [1])
     for h in range(1, heads - 1):
         send_own(h, range(PIECES))
     for copy in stages[4:]:
@@ -273,20 +271,21 @@
         acc[h, HDIM:, :] = rescale * acc[h, HDIM:, :] + both[HDIM:] + moved
 
     def finish(h):
-        sums = stats[h, 1:2, :]
-        inverse = jnp.where(sums > 0.0, 1.0 / jnp.where(sums > 0.0, sums, 1.0), 0.0)
-        mean = stats[h, 2:3, :] * inverse
-        primal = acc[h, 0:HDIM, :] * inverse
-        tangent = acc[h, HDIM:, :] * inverse - mean * primal
-        own_o[h, 0:HDIM, :] = primal[:, :rows]
-        own_o[h, HDIM:, :] = tangent[:, :rows]
-        o_send[h, 0:HDIM, :] = primal[:, rows:].astype(jnp.bfloat16)
-        o_send[h, HDIM:, :] = tangent[:, rows:].astype(jnp.bfloat16)
-        for i, row in enumerate((stats[h, 0:1, :], sums, mean)):
-            own_stats[h, i : i + 1, :] = row[:, :rows]
-            s_send[h, i : i + 1, :] = row[:, rows:]
-        for copy in o_copies(h):
-            copy.start()
+        for slot in (1, 0):
+            lanes = slice(slot * rows, (slot + 1) * rows)
+            sums = stats[h, 1:2, lanes]
+            inverse = jnp.where(sums > 0.0, 1.0 / jnp.where(sums > 0.0, sums, 1.0), 0.0)
+            mean = stats[h, 2:3, lanes] * inverse
+            primal = acc[h, 0:HDIM, lanes] * inverse
+            tangent = acc[h, HDIM:, lanes] * inverse - mean * primal
+            out_ref, stats_ref = ((own_o, own_stats), (o_send, s_send))[slot]
+            out_ref[h, 0:HDIM, :] = primal.astype(out_ref.dtype)
+            out_ref[h, HDIM:, :] = tangent.astype(out_ref.dtype)
+            for i, row in enumerate((stats[h, 0:1, lanes], sums, mean)):
+                stats_ref[h, i : i + 1, :] = row
+            if slot == 1:
+                for copy in o_copies(h):
+                    copy.start()
 
     def merge(h):
         for copy in o_copies(h):
@@ -339,7 +338,7 @@
 
     def forward(h, d, piece):
         for side in range(2):
-            crosses = (piece < 2) == (side == 0)
+            crosses = piece == side
 
             def take(side=side, crosses=crosses):
                 arrived = ring_copy(h, d - 1, piece, side)
@@ -388,11 +387,6 @@
             @pl.when(old_d == depth)
             def _():
                 finish(old_h)
-
-        @pl.when(live)
-        def _():
-            for piece in range(2, PIECES):
-                forward(h, d, piece)
 
         @pl.when(index == late - 2)
         def _():

time: 101 us -> 103 us (1.020)
  Pallas kernels: 98.5 us -> 100 us
    pallas_call x1, Pallas kernels: 98.5 us -> 100 us  [local(): pl.pallas_call(functools.partial(kernel, nz, n_head), out_shape=jax.Shape...]
where the time goes in v6:
time: 103 us
  Pallas kernels  100 us (97%)
  local copies, waits for them, and re-layouts  1.75 us (2%)
    pallas_call x1, Pallas kernels, local(): pl.pallas_call(functools.partial(kernel, nz, n_head), out_shape=jax.Shape...  100 us

profile of v6, /device:TPU:2, one launch (start us, length us, event | category | flops | bytes accessed | tf_op | source)
XLA Modules:
  0.0 102.8 jit_solution(18367234290985169011)
XLA Ops:
  0.6 100.4 %shard_map.104 = bf16[256,640]{1,0:T(8,128)(2,1)} custom-call(bf16[128,384]{1,0:T(8,128)(2,1)} %q_in.1, bf16[128,384]{1,0:T(8,128)(2,1)} %k_in.1, bf16[128,384]{1,0:T(8,128)(2,1)} %v_in.1, bf16[128,384]{1,0:T(8,128)(2,1)} %tq_in.1, bf16[128,384]{1,0:T(8,128)(2,1)} %tk_in.1, bf16[128,384]{1,0:T(8,128)(2,1)} %tv_in.1, bf16[3,128,5120]{2,1,0:T(8,128)(2,1)} %bitcast.1, ...), custom_call_target="tpu_custom_call" | custom-call | flops 3422552064 | bytes 8388608 | tf_op jit(solution)/shard_map/pallas_call | solution.py:442
  101.0 1.7 %fusion = (bf16[128,640]{1,0:T(8,128)(2,1)}, bf16[128,640]{1,0:T(8,128)(2,1)}) fusion(bf16[256,640]{1,0:T(8,128)(2,1)} %shard_map.104), kind=kLoop, calls=%fused_computation | loop fusion | bytes 655360 | tf_op jit(solution)/shard_map/slice | solution.py:499

commit v7 on v6

--- a/solution.py
+++ b/solution.py
@@ -1,4 +1,5 @@
 import functools
+import math
 
 import jax
 import jax.numpy as jnp
@@ -8,7 +9,7 @@
 from jax.sharding import PartitionSpec as P
 
 HDIM = 128
-PIECES = 2
+PIECES = 4
 NONE_SEEN = -1e29
 MASKED = -1e30
 
@@ -17,8 +18,15 @@
     return lax.dot_general(a, b, (((1,), (0,)), ((), ())), preferred_element_type=jnp.float32)
 
 
-def dot_nt(a, b):
-    return lax.dot_general(a, b, (((1,), (1,)), ((), ())), preferred_element_type=jnp.float32)
+def turned(block):
+    return block.astype(jnp.float32).T.astype(jnp.bfloat16)
+
+
+def schedule(heads, depth):
+    if heads != 3 or depth != 8:
+        return [(h, d) for d in range(1, depth + 1) for h in range(heads)]
+    turns = [0, 1, 0, 2] * 3 + [0, 1] * 2 + [2, 1] * 3 + [2, 2]
+    return [(h, turns[: i + 1].count(h)) for i, h in enumerate(turns)]
 
 
 def kernel(
@@ -131,7 +139,9 @@
     def ring_copy(h, hop, piece, side):
         source = (z + nz - hop) % nz if side == 0 else (z + hop) % nz
         step = h * depth + hop
-        ref = (kbuf, vbuf)[piece].at[h, source]
+        buf = kbuf if piece < 2 else vbuf
+        size = buf.shape[2] // 2
+        ref = buf.at[h, source, pl.ds((piece % 2) * size, size), :]
         return pltpu.make_async_remote_copy(
             src_ref=ref,
             dst_ref=ref,
@@ -207,20 +217,20 @@
         kbuf[h, z, :, 0:HDIM] = stage[0, :, cols]
         kbuf[h, z, :, HDIM : 2 * HDIM] = stage[1, :, cols]
     pl.semaphore_wait(barrier, 3 + n_head)
-    send_own(0, [0])
+    send_own(0, range(2))
     for copy in stages[2:4]:
         copy.wait()
     for h, cols in enumerate(columns):
-        vbuf[h, z, 0:HDIM, :] = stage[2, :, cols].astype(jnp.float32).T.astype(jnp.bfloat16)
-        vbuf[h, z, HDIM : 2 * HDIM, :] = stage[3, :, cols].astype(jnp.float32).T.astype(jnp.bfloat16)
-    send_own(0, [1])
-    for h in range(1, heads - 1):
+        vbuf[h, z, 0:HDIM, :] = turned(stage[2, :, cols])
+        vbuf[h, z, HDIM : 2 * HDIM, :] = turned(stage[3, :, cols])
+    send_own(0, range(2, PIECES))
+    for h in range(1, heads):
         send_own(h, range(PIECES))
     for copy in stages[4:]:
         copy.wait()
     for h, cols in enumerate(columns):
-        qbuf[0, h, :, HDIM : 2 * HDIM] = stage[4, :, cols]
-        qbuf[0, h, :, 0:HDIM] = stage[5, :, cols]
+        qbuf[0, h, 0:HDIM, :] = turned(stage[5, :, cols])
+        qbuf[0, h, HDIM : 2 * HDIM, :] = turned(stage[4, :, cols])
         q_copy(h).start()
     for i in range(1, n_head):
         w_copy(i).start()
@@ -239,9 +249,9 @@
 
     def score(h, first, second):
         key = jnp.concatenate([kbuf[h, first], kbuf[h, second]], axis=0)
-        query = jnp.concatenate([qbuf[0, h], qbuf[1, h]], axis=0)
-        scores = dot_nt(key[:, :HDIM], query[:, HDIM:]) * scale
-        tan_scores = dot_nt(key, query) * scale
+        query = jnp.concatenate([qbuf[0, h], qbuf[1, h]], axis=1)
+        scores = dot(key[:, :HDIM], query[HDIM:]) * (scale * math.log2(math.e))
+        tan_scores = dot(key, query)
         masks = allowed_keys(first) + allowed_keys(second)
         masked = jnp.concatenate(
             [
@@ -252,12 +262,14 @@
         )
         peak = stats[h, 0:1, :]
         new_peak = jnp.maximum(peak, jnp.max(masked, axis=0, keepdims=True))
-        weights = jnp.exp(masked - new_peak)
-        rescale = jnp.exp(peak - new_peak)
+        weights = jnp.exp2(masked - new_peak)
+        rescale = jnp.exp2(peak - new_peak)
         products = weights * tan_scores
         stats[h, 0:1, :] = new_peak
         stats[h, 1:2, :] = rescale * stats[h, 1:2, :] + jnp.sum(weights, axis=0, keepdims=True)
-        stats[h, 2:3, :] = rescale * stats[h, 2:3, :] + jnp.sum(products, axis=0, keepdims=True)
+        stats[h, 2:3, :] = rescale * stats[h, 2:3, :] + scale * jnp.sum(
+            products, axis=0, keepdims=True
+        )
         stats[h, 3:4, :] = rescale
         factors[0] = weights.astype(jnp.bfloat16)
         factors[1] = products.astype(jnp.bfloat16)
@@ -268,7 +280,7 @@
         moved = dot(value[:HDIM], factors[1])
         rescale = stats[h, 3:4, :]
         acc[h, 0:HDIM, :] = rescale * acc[h, 0:HDIM, :] + both[:HDIM]
-        acc[h, HDIM:, :] = rescale * acc[h, HDIM:, :] + both[HDIM:] + moved
+        acc[h, HDIM:, :] = rescale * acc[h, HDIM:, :] + both[HDIM:] + scale * moved
 
     def finish(h):
         for slot in (1, 0):
@@ -296,7 +308,7 @@
             sums.append(ref[h, 1:2, :])
             means.append(ref[h, 2:3, :])
         peak = jnp.maximum(peaks[0], peaks[1])
-        shares = [sums[i] * jnp.exp(peaks[i] - peak) for i in range(2)]
+        shares = [sums[i] * jnp.exp2(peaks[i] - peak) for i in range(2)]
         inverse = 1.0 / (shares[0] + shares[1])
         shares = [share * inverse for share in shares]
         mean = shares[0] * means[0] + shares[1] * means[1]
@@ -312,33 +324,35 @@
             g_copy(h, i).start()
 
     def project(h):
-        for i in range(1, n_head):
-            g_copy(h, i).wait()
-        features = jnp.concatenate([gbuf[h, g] for g in range(n_head)], axis=1)
-        total[...] += dot(features, wbuf[h])
-
-    mid = 3 * depth // 2
-    late = mid + depth
-    steps = heads * depth
+        for first in range(0, n_head, 2):
+            sources = [(hd + n_head - i) % n_head for i in (first, first + 1)]
+            for i in (first, first + 1):
+                if i > 0:
+                    g_copy(h, i).wait()
+            features = jnp.concatenate([gbuf[h, source] for source in sources], axis=1)
+            weight = jnp.concatenate(
+                [
+                    wbuf[h, pl.ds(pl.multiple_of(source * HDIM, HDIM), HDIM), :]
+                    for source in sources
+                ],
+                axis=0,
+            )
+            total[...] += dot(features, weight)
+
+    order_of = schedule(heads, depth)
+    steps = len(order_of)
+    finished = [order_of.index((h, depth)) for h in range(heads)]
 
     def place(index):
-        group, turn = index // 3, index % 3
-        slow = turn % 2
-        h_a = slow
-        d_a = (1 - slow) * (2 * group + turn // 2 + 1) + slow * (group + 1)
-        pair, new = (index - mid) // 2, (index - mid) % 2
-        h_b = 1 + new
-        d_b = pair + 1 + (1 - new) * (depth // 2)
-        d_c = depth // 2 + index - late + 1
-        past_mid = jnp.minimum(index // mid, 1)
-        past_late = jnp.minimum(index // late, 1)
-        h = (1 - past_mid) * h_a + (past_mid - past_late) * h_b + past_late * 2
-        d = (1 - past_mid) * d_a + (past_mid - past_late) * d_b + past_late * d_c
+        h = d = 0
+        for i, (head_at, hop_at) in enumerate(order_of):
+            h = h + jnp.where(index == i, head_at, 0)
+            d = d + jnp.where(index == i, hop_at, 0)
         return h, d
 
     def forward(h, d, piece):
         for side in range(2):
-            crosses = piece == side
+            crosses = (piece < 2) == (side == 0)
 
             def take(side=side, crosses=crosses):
                 arrived = ring_copy(h, d - 1, piece, side)
@@ -357,7 +371,7 @@
 
     def step(index, carry):
         h, d = place(index)
-        old_h, old_d = place(jnp.maximum(index - 1, 0))
+        old_h, old_d = carry
         first, second = (z + nz - old_d) % nz, (z + old_d % depth) % nz
         live = index < steps
 
@@ -388,25 +402,26 @@
             def _():
                 finish(old_h)
 
-        @pl.when(index == late - 2)
+        @pl.when(live)
+        def _():
+            for piece in range(2, PIECES):
+                forward(h, d, piece)
+
+        @pl.when(index == min(finished[0] + 2, steps))
         def _():
             for i in range(1, n_head):
                 w_copy(i).wait()
                 w_share(i).start()
 
-        @pl.when(jnp.logical_and(d == depth - 1, h == 0))
-        def _():
-            send_own(heads - 1, range(PIECES))
-
-        for early, when in ((0, mid + 2), (1, late + 1)):
-
-            @pl.when(index == when)
+        for early in range(heads - 1):
+
+            @pl.when(index == min(finished[early] + 3, steps))
             def _(early=early):
                 merge(early)
 
-        return carry
-
-    lax.fori_loop(0, steps + 1, step, 0)
+        return h, d
+
+    lax.fori_loop(0, steps + 1, step, (jnp.int32(0), jnp.int32(1)))
     own_w.wait()
     for i in range(1, n_head):
         w_share(i).wait()
@@ -448,7 +463,7 @@
             pltpu.SMEM(clip_lengths.shape, jnp.int32),
             pltpu.SMEM(stretch_order.shape, jnp.int32),
             pltpu.VMEM((6, rows, width), bf16),
-            pltpu.VMEM((2, heads, rows, 2 * HDIM), bf16),
+            pltpu.VMEM((2, heads, 2 * HDIM, rows), bf16),
             pltpu.VMEM((heads, nz, rows, 2 * HDIM), bf16),
             pltpu.VMEM((heads, nz, 2 * HDIM, rows), bf16),
             pltpu.VMEM((heads, n_head * HDIM, ncol), bf16),

time: 103 us -> 101 us (0.981)
  Pallas kernels: 100 us -> 98 us
    pallas_call x1, Pallas kernels: 100 us -> 98 us  [local(): pl.pallas_call(functools.partial(kernel, nz, n_head), out_shape=jax.Shape...]
where the time goes in v7:
time: 101 us; the launch traced here: 100 us
  Pallas kernels  98 us (97%)
  local copies, waits for them, and re-layouts  1.75 us (2%)
    pallas_call x1, Pallas kernels, local(): pl.pallas_call(functools.partial(kernel, nz, n_head), out_shape=jax.Shape...  98 us

profile of v7, /device:TPU:2, one launch (start us, length us, event | category | flops | bytes accessed | tf_op | source)
XLA Modules:
  0.0 100.4 jit_solution(8091650535277618267)
XLA Ops:
  0.6 98.0 %shard_map.104 = bf16[256,640]{1,0:T(8,128)(2,1)} custom-call(bf16[128,384]{1,0:T(8,128)(2,1)} %q_in.1, bf16[128,384]{1,0:T(8,128)(2,1)} %k_in.1, bf16[128,384]{1,0:T(8,128)(2,1)} %v_in.1, bf16[128,384]{1,0:T(8,128)(2,1)} %tq_in.1, bf16[128,384]{1,0:T(8,128)(2,1)} %tk_in.1, bf16[128,384]{1,0:T(8,128)(2,1)} %tv_in.1, bf16[3,128,5120]{2,1,0:T(8,128)(2,1)} %bitcast.1, ...), custom_call_target="tpu_custom_call" | custom-call | flops 3422552064 | bytes 8388608 | tf_op jit(solution)/shard_map/pallas_call | solution.py:457
  98.7 1.7 %fusion = (bf16[128,640]{1,0:T(8,128)(2,1)}, bf16[128,640]{1,0:T(8,128)(2,1)}) fusion(bf16[256,640]{1,0:T(8,128)(2,1)} %shard_map.104), kind=kLoop, calls=%fused_computation | loop fusion | bytes 655360 | tf_op jit(solution)/shard_map/slice | solution.py:514

commit v8 on v7

--- a/solution.py
+++ b/solution.py
@@ -25,7 +25,7 @@
 def schedule(heads, depth):
     if heads != 3 or depth != 8:
         return [(h, d) for d in range(1, depth + 1) for h in range(heads)]
-    turns = [0, 1, 0, 2] * 3 + [0, 1] * 2 + [2, 1] * 3 + [2, 2]
+    turns = [0, 1, 0, 2] * 3 + [0, 1] * 2 + [1, 2] * 3 + [2, 2]
     return [(h, turns[: i + 1].count(h)) for i, h in enumerate(turns)]
 
 
@@ -247,12 +247,12 @@
             parts.append(jnp.logical_and(position >= low - first, position < high - first))
         return parts
 
-    def score(h, first, second):
-        key = jnp.concatenate([kbuf[h, first], kbuf[h, second]], axis=0)
+    def score(h, sources):
+        key = jnp.concatenate([kbuf[h, source] for source in sources], axis=0)
         query = jnp.concatenate([qbuf[0, h], qbuf[1, h]], axis=1)
         scores = dot(key[:, :HDIM], query[HDIM:]) * (scale * math.log2(math.e))
         tan_scores = dot(key, query)
-        masks = allowed_keys(first) + allowed_keys(second)
+        masks = [mask for source in sources for mask in allowed_keys(source)]
         masked = jnp.concatenate(
             [
                 jnp.where(mask, scores[i * half : (i + 1) * half], MASKED)
@@ -271,13 +271,15 @@
             products, axis=0, keepdims=True
         )
         stats[h, 3:4, :] = rescale
-        factors[0] = weights.astype(jnp.bfloat16)
-        factors[1] = products.astype(jnp.bfloat16)
-
-    def apply(h, first, second):
-        value = jnp.concatenate([vbuf[h, first], vbuf[h, second]], axis=1)
-        both = dot(value, factors[0])
-        moved = dot(value[:HDIM], factors[1])
+        span = len(sources) * rows
+        factors[0, 0:span] = weights.astype(jnp.bfloat16)
+        factors[1, 0:span] = products.astype(jnp.bfloat16)
+
+    def apply(h, sources):
+        value = jnp.concatenate([vbuf[h, source] for source in sources], axis=1)
+        span = len(sources) * rows
+        both = dot(value, factors[0, 0:span])
+        moved = dot(value[:HDIM], factors[1, 0:span])
         rescale = stats[h, 3:4, :]
         acc[h, 0:HDIM, :] = rescale * acc[h, 0:HDIM, :] + both[:HDIM]
         acc[h, HDIM:, :] = rescale * acc[h, HDIM:, :] + both[HDIM:] + scale * moved
@@ -372,7 +374,7 @@
     def step(index, carry):
         h, d = place(index)
         old_h, old_d = carry
-        first, second = (z + nz - old_d) % nz, (z + old_d % depth) % nz
+        far, near = [(z + nz - old_d) % nz], [(z + nz - old_d) % nz, (z + old_d) % nz]
         live = index < steps
 
         @pl.when(live)
@@ -387,8 +389,16 @@
                 stats[old_h, 1:3, :] = jnp.zeros((2, 2 * rows), jnp.float32)
                 acc[old_h] = jnp.zeros((2 * HDIM, 2 * rows), jnp.float32)
                 q_copy(old_h).wait()
-
-            score(old_h, first, second)
+                score(old_h, [z])
+                apply(old_h, [z])
+
+            @pl.when(old_d < depth)
+            def _():
+                score(old_h, near)
+
+            @pl.when(old_d == depth)
+            def _():
+                score(old_h, far)
 
         @pl.when(live)
         def _():
@@ -396,10 +406,13 @@
 
         @pl.when(index > 0)
         def _():
-            apply(old_h, first, second)
+            @pl.when(old_d < depth)
+            def _():
+                apply(old_h, near)
 
             @pl.when(old_d == depth)
             def _():
+                apply(old_h, far)
                 finish(old_h)
 
         @pl.when(live)
@@ -415,7 +428,7 @@
 
         for early in range(heads - 1):
 
-            @pl.when(index == min(finished[early] + 3, steps))
+            @pl.when(index == min(finished[early] + 2, steps))
             def _(early=early):
                 merge(early)
 
@@ -456,7 +469,7 @@
     in_vmem = pl.BlockSpec(memory_space=pltpu.VMEM)
     both = pl.pallas_call(
         functools.partial(kernel, nz, n_head),
-        out_shape=jax.ShapeDtypeStruct((2 * rows, ncol), bf16),
+        out_shape=pltpu.VMEM((2 * rows, ncol), bf16),
         in_specs=[anywhere] * 9,
         out_specs=in_vmem,
         scratch_shapes=[

time: 101 us -> 99.5 us (0.985)
  no operation moved by 1% of the time
where the time goes in v8:
time: 99.5 us; the launch traced here: 99.4 us
  Pallas kernels  98 us (98%)
    pallas_call x1, Pallas kernels, local(): pl.pallas_call(functools.partial(kernel, nz, n_head), out_shape=pltpu.VME...  98 us

profile of v8, /device:TPU:2, one launch (start us, length us, event | category | flops | bytes accessed | tf_op | source)
XLA Modules:
  0.0 99.4 jit_solution(14800849962729026242)
XLA Ops:
  0.6 98.0 %shard_map.104 = bf16[256,640]{1,0:T(8,128)(2,1)S(1)} custom-call(bf16[128,384]{1,0:T(8,128)(2,1)} %q_in.1, bf16[128,384]{1,0:T(8,128)(2,1)} %k_in.1, bf16[128,384]{1,0:T(8,128)(2,1)} %v_in.1, bf16[128,384]{1,0:T(8,128)(2,1)} %tq_in.1, bf16[128,384]{1,0:T(8,128)(2,1)} %tk_in.1, bf16[128,384]{1,0:T(8,128)(2,1)} %tv_in.1, bf16[3,128,5120]{2,1,0:T(8,128)(2,1)} %bitcast.1, ...), custom_call_target="tpu_custom_call" | custom-call | flops 3422552064 | bytes 8388608 | tf_op jit(solution)/shard_map/pallas_call | solution.py:470
  98.6 0.8 fusion

commit v9 on v8

--- a/solution.py
+++ b/solution.py
@@ -352,75 +352,54 @@
             d = d + jnp.where(index == i, hop_at, 0)
         return h, d
 
-    def forward(h, d, piece):
-        for side in range(2):
-            crosses = (piece < 2) == (side == 0)
-
-            def take(side=side, crosses=crosses):
-                arrived = ring_copy(h, d - 1, piece, side)
-                arrived.wait_recv()
-
-                @pl.when(d < depth if crosses else d < depth - 1)
-                def _():
-                    ring_copy(h, d, piece, side).start()
-
-                arrived.wait_send()
-
-            if crosses:
-                take()
-            else:
-                pl.when(d < depth)(take)
+    def each_piece(d, act):
+        for piece in range(PIECES):
+            for side in range(2):
+                crosses = (piece < 2) == (side == 0)
+                if crosses:
+                    act(piece, side, d < depth)
+                else:
+                    pl.when(d < depth)(functools.partial(act, piece, side, d < depth - 1))
 
     def step(index, carry):
         h, d = place(index)
-        old_h, old_d = carry
-        far, near = [(z + nz - old_d) % nz], [(z + nz - old_d) % nz, (z + old_d) % nz]
-        live = index < steps
-
-        @pl.when(live)
+        far, near = [(z + nz - d) % nz], [(z + nz - d) % nz, (z + d) % nz]
+
+        def forward(piece, side, goes_on):
+            ring_copy(h, d - 1, piece, side).wait_recv()
+
+            @pl.when(goes_on)
+            def _():
+                ring_copy(h, d, piece, side).start()
+
+        def settle(piece, side, goes_on):
+            ring_copy(h, d - 1, piece, side).wait_send()
+
+        each_piece(d, forward)
+
+        @pl.when(d == 1)
         def _():
-            forward(h, d, 0)
-
-        @pl.when(index > 0)
+            stats[h, 0:1, :] = jnp.full((1, 2 * rows), NONE_SEEN, jnp.float32)
+            stats[h, 1:3, :] = jnp.zeros((2, 2 * rows), jnp.float32)
+            acc[h] = jnp.zeros((2 * HDIM, 2 * rows), jnp.float32)
+            q_copy(h).wait()
+            score(h, [z])
+            apply(h, [z])
+
+        @pl.when(d < depth)
         def _():
-            @pl.when(old_d == 1)
-            def _():
-                stats[old_h, 0:1, :] = jnp.full((1, 2 * rows), NONE_SEEN, jnp.float32)
-                stats[old_h, 1:3, :] = jnp.zeros((2, 2 * rows), jnp.float32)
-                acc[old_h] = jnp.zeros((2 * HDIM, 2 * rows), jnp.float32)
-                q_copy(old_h).wait()
-                score(old_h, [z])
-                apply(old_h, [z])
-
-            @pl.when(old_d < depth)
-            def _():
-                score(old_h, near)
-
-            @pl.when(old_d == depth)
-            def _():
-                score(old_h, far)
-
-        @pl.when(live)
+            score(h, near)
+            apply(h, near)
+
+        @pl.when(d == depth)
         def _():
-            forward(h, d, 1)
-
-        @pl.when(index > 0)
-        def _():
-            @pl.when(old_d < depth)
-            def _():
-                apply(old_h, near)
-
-            @pl.when(old_d == depth)
-            def _():
-                apply(old_h, far)
-                finish(old_h)
-
-        @pl.when(live)
-        def _():
-            for piece in range(2, PIECES):
-                forward(h, d, piece)
-
-        @pl.when(index == min(finished[0] + 2, steps))
+            score(h, far)
+            apply(h, far)
+            finish(h)
+
+        each_piece(d, settle)
+
+        @pl.when(index == min(finished[0] + 2, steps - 1))
         def _():
             for i in range(1, n_head):
                 w_copy(i).wait()
@@ -428,13 +407,13 @@
 
         for early in range(heads - 1):
 
-            @pl.when(index == min(finished[early] + 2, steps))
+            @pl.when(index == min(finished[early] + 1, steps - 1))
             def _(early=early):
                 merge(early)
 
-        return h, d
-
-    lax.fori_loop(0, steps + 1, step, (jnp.int32(0), jnp.int32(1)))
+        return carry
+
+    lax.fori_loop(0, steps, step, 0)
     own_w.wait()
     for i in range(1, n_head):
         w_share(i).wait()

time: 99.5 us -> 99.7 us (level)
  no operation moved by 1% of the time
where the time goes in v9:
time: 99.7 us; the launch traced here: 99.6 us
  Pallas kernels  98.2 us (98%)
    pallas_call x1, Pallas kernels, local(): pl.pallas_call(functools.partial(kernel, nz, n_head), out_shape=pltpu.VME...  98.2 us

profile of v9, /device:TPU:2, one launch (start us, length us, event | category | flops | bytes accessed | tf_op | source)
XLA Modules:
  0.0 99.6 jit_solution(818438875601873815)
XLA Ops:
  0.6 98.2 %shard_map.104 = bf16[256,640]{1,0:T(8,128)(2,1)S(1)} custom-call(bf16[128,384]{1,0:T(8,128)(2,1)} %q_in.1, bf16[128,384]{1,0:T(8,128)(2,1)} %k_in.1, bf16[128,384]{1,0:T(8,128)(2,1)} %v_in.1, bf16[128,384]{1,0:T(8,128)(2,1)} %tq_in.1, bf16[128,384]{1,0:T(8,128)(2,1)} %tk_in.1, bf16[128,384]{1,0:T(8,128)(2,1)} %tv_in.1, bf16[3,128,5120]{2,1,0:T(8,128)(2,1)} %bitcast.1, ...), custom_call_target="tpu_custom_call" | custom-call | flops 3422552064 | bytes 8388608 | tf_op jit(solution)/shard_map/pallas_call | solution.py:449
  98.8 0.8 fusion

commit v10 on v8

--- a/solution.py
+++ b/solution.py
@@ -114,28 +114,6 @@
         pl.semaphore_signal(barrier, inc=1, device_id={"head": (hd + i) % n_head})
     pl.semaphore_signal(barrier, inc=1, device_id={"dp": 1 - core})
 
-    for copy in tables:
-        copy.wait()
-    ends = []
-    running = jnp.int32(0)
-    for c in range(clips):
-        running = running + lengths[c]
-        ends.append(running)
-    lane = lax.broadcasted_iota(jnp.int32, (1, rows), 1)
-    for slot, index in enumerate((ctx, partner)):
-        anchor = jnp.where(
-            lane < half,
-            order[2 * index] * half + lane,
-            order[2 * index + 1] * half + lane - half,
-        )
-        low = jnp.zeros_like(anchor)
-        high = jnp.full_like(anchor, rows * nz * 2)
-        for end in ends:
-            low = jnp.where(end <= anchor, jnp.maximum(low, end), low)
-            high = jnp.where(end > anchor, jnp.minimum(high, end), high)
-        bounds[0:1, slot * rows : (slot + 1) * rows] = low
-        bounds[1:2, slot * rows : (slot + 1) * rows] = high
-
     def ring_copy(h, hop, piece, side):
         source = (z + nz - hop) % nz if side == 0 else (z + hop) % nz
         step = h * depth + hop
@@ -201,14 +179,32 @@
             for src, dst, sem in ((s_send, s_recv, s_sem), (o_send, o_recv, o_sem))
         ]
 
-    def g_copy(h, i):
+    n_y = n_head // 2
+    y, x = hd // 2, hd % 2
+    relayed = n_head // 2 + 1 if n_y == 4 else 0
+    direct = [k for k in range(1, n_head) if k != relayed]
+    direct.sort(key=lambda k: -min(k // 2, n_y - k // 2))
+
+    def target(k):
+        return (y + k // 2) % n_y * 2 + (x + k) % 2
+
+    def source(k):
+        return (y + n_y - k // 2) % n_y * 2 + (x + k) % 2
+
+    def g_copy(h, k):
+        block = hd if k != relayed else source(relayed - 1)
         return pltpu.make_async_remote_copy(
-            src_ref=gbuf.at[h, hd],
-            dst_ref=gbuf.at[h, hd],
-            send_sem=g_send.at[h, i - 1],
-            recv_sem=g_recv.at[h, i - 1],
-            device_id={"head": (hd + i) % n_head},
-        )
+            src_ref=gbuf.at[h, block],
+            dst_ref=gbuf.at[h, block],
+            send_sem=g_send.at[h, k - 1],
+            recv_sem=g_recv.at[h, k - 1],
+            device_id={"head": target(k if k != relayed else 1)},
+        )
+
+    def relay(h):
+        if relayed:
+            g_copy(h, relayed - 1).wait()
+            g_copy(h, relayed).start()
 
     columns = [slice(h * HDIM, (h + 1) * HDIM) for h in range(heads)]
     for copy in stages[:2]:
@@ -234,6 +230,28 @@
         q_copy(h).start()
     for i in range(1, n_head):
         w_copy(i).start()
+    for copy in tables:
+        copy.wait()
+    ends = []
+    running = jnp.int32(0)
+    for c in range(clips):
+        running = running + lengths[c]
+        ends.append(running)
+    lane = lax.broadcasted_iota(jnp.int32, (1, rows), 1)
+    for slot, index in enumerate((ctx, partner)):
+        anchor = jnp.where(
+            lane < half,
+            order[2 * index] * half + lane,
+            order[2 * index + 1] * half + lane - half,
+        )
+        low = jnp.zeros_like(anchor)
+        high = jnp.full_like(anchor, rows * nz * 2)
+        for end in ends:
+            low = jnp.where(end <= anchor, jnp.maximum(low, end), low)
+            high = jnp.where(end > anchor, jnp.minimum(high, end), high)
+        bounds[0:1, slot * rows : (slot + 1) * rows] = low
+        bounds[1:2, slot * rows : (slot + 1) * rows] = high
+
     total[...] = jnp.zeros_like(total)
     s_send[...] = jnp.zeros_like(s_send)
 
@@ -322,21 +340,20 @@
         )
         gbuf[h, hd, 0:rows, :] = primal.T.astype(jnp.bfloat16)
         gbuf[h, hd, rows:, :] = tangent.T.astype(jnp.bfloat16)
-        for i in range(1, n_head):
-            g_copy(h, i).start()
+        for k in direct:
+            g_copy(h, k).start()
 
     def project(h):
+        arrivals = [0] + direct[::-1] + ([relayed] if relayed else [])
         for first in range(0, n_head, 2):
-            sources = [(hd + n_head - i) % n_head for i in (first, first + 1)]
-            for i in (first, first + 1):
-                if i > 0:
-                    g_copy(h, i).wait()
-            features = jnp.concatenate([gbuf[h, source] for source in sources], axis=1)
+            pair = arrivals[first : first + 2]
+            for k in pair:
+                if k > 0 and k != relayed - 1:
+                    g_copy(h, k).wait()
+            sources = [source(k) for k in pair]
+            features = jnp.concatenate([gbuf[h, g] for g in sources], axis=1)
             weight = jnp.concatenate(
-                [
-                    wbuf[h, pl.ds(pl.multiple_of(source * HDIM, HDIM), HDIM), :]
-                    for source in sources
-                ],
+                [wbuf[h, pl.ds(pl.multiple_of(g * HDIM, HDIM), HDIM), :] for g in sources],
                 axis=0,
             )
             total[...] += dot(features, weight)
@@ -432,14 +449,21 @@
             def _(early=early):
                 merge(early)
 
+        @pl.when(index == min(finished[0] + 5, steps))
+        def _():
+            relay(0)
+
         return h, d
 
     lax.fori_loop(0, steps + 1, step, (jnp.int32(0), jnp.int32(1)))
     own_w.wait()
     for i in range(1, n_head):
         w_share(i).wait()
+    for h in range(1, heads - 1):
+        relay(h)
     project(0)
     merge(heads - 1)
+    relay(heads - 1)
     for h in range(1, heads):
         project(h)
     out[...] = total[...].astype(out.dtype)

time: 99.5 us -> 100 us (level)
  Pallas kernels: 98 us -> 99 us
where the time goes in v10:
time: 100 us
  Pallas kernels  99 us (99%)
    pallas_call x1, Pallas kernels, local(): pl.pallas_call(functools.partial(kernel, nz, n_head), out_shape=pltpu.VME...  99 us

profile of v10, /device:TPU:2, one launch (start us, length us, event | category | flops | bytes accessed | tf_op | source)
XLA Modules:
  0.0 100.4 jit_solution(4108321713565275160)
XLA Ops:
  0.6 99.0 %shard_map.104 = bf16[256,640]{1,0:T(8,128)(2,1)S(1)} custom-call(bf16[128,384]{1,0:T(8,128)(2,1)} %q_in.1, bf16[128,384]{1,0:T(8,128)(2,1)} %k_in.1, bf16[128,384]{1,0:T(8,128)(2,1)} %v_in.1, bf16[128,384]{1,0:T(8,128)(2,1)} %tq_in.1, bf16[128,384]{1,0:T(8,128)(2,1)} %tk_in.1, bf16[128,384]{1,0:T(8,128)(2,1)} %tv_in.1, bf16[3,128,5120]{2,1,0:T(8,128)(2,1)} %bitcast.1, ...), custom_call_target="tpu_custom_call" | custom-call | flops 3422552064 | bytes 8388608 | tf_op jit(solution)/shard_map/pallas_call | solution.py:494
  99.6 0.8 fusion

commit v11 on v8

--- a/solution.py
+++ b/solution.py
@@ -224,8 +224,12 @@
         vbuf[h, z, 0:HDIM, :] = turned(stage[2, :, cols])
         vbuf[h, z, HDIM : 2 * HDIM, :] = turned(stage[3, :, cols])
     send_own(0, range(2, PIECES))
-    for h in range(1, heads):
-        send_own(h, range(PIECES))
+
+    @pl.when(core == 0)
+    def _():
+        for h in range(1, heads):
+            send_own(h, range(PIECES))
+
     for copy in stages[4:]:
         copy.wait()
     for h, cols in enumerate(columns):
@@ -419,6 +423,11 @@
         def _():
             for piece in range(2, PIECES):
                 forward(h, d, piece)
+
+        @pl.when(jnp.logical_and(index == 0, core != 0))
+        def _():
+            for other in range(1, heads):
+                send_own(other, range(PIECES))
 
         @pl.when(index == min(finished[0] + 2, steps))
         def _():

time: 99.5 us -> 98.8 us (level)
  no operation moved by 1% of the time
where the time goes in v11:
time: 98.8 us; the launch traced here: 98.6 us
  Pallas kernels  97.3 us (98%)
    pallas_call x1, Pallas kernels, local(): pl.pallas_call(functools.partial(kernel, nz, n_head), out_shape=pltpu.VME...  97.3 us

profile of v11, /device:TPU:2, one launch (start us, length us, event | category | flops | bytes accessed | tf_op | source)
XLA Modules:
  0.0 98.6 jit_solution(11860132974457775813)
XLA Ops:
  0.6 97.3 %shard_map.104 = bf16[256,640]{1,0:T(8,128)(2,1)S(1)} custom-call(bf16[128,384]{1,0:T(8,128)(2,1)} %q_in.1, bf16[128,384]{1,0:T(8,128)(2,1)} %k_in.1, bf16[128,384]{1,0:T(8,128)(2,1)} %v_in.1, bf16[128,384]{1,0:T(8,128)(2,1)} %tq_in.1, bf16[128,384]{1,0:T(8,128)(2,1)} %tk_in.1, bf16[128,384]{1,0:T(8,128)(2,1)} %tv_in.1, bf16[3,128,5120]{2,1,0:T(8,128)(2,1)} %bitcast.1, ...), custom_call_target="tpu_custom_call" | custom-call | flops 3422552064 | bytes 8388608 | tf_op jit(solution)/shard_map/pallas_call | solution.py:479
  97.9 0.8 fusion

commit v12 on v11

--- a/solution.py
+++ b/solution.py
@@ -114,28 +114,6 @@
         pl.semaphore_signal(barrier, inc=1, device_id={"head": (hd + i) % n_head})
     pl.semaphore_signal(barrier, inc=1, device_id={"dp": 1 - core})
 
-    for copy in tables:
-        copy.wait()
-    ends = []
-    running = jnp.int32(0)
-    for c in range(clips):
-        running = running + lengths[c]
-        ends.append(running)
-    lane = lax.broadcasted_iota(jnp.int32, (1, rows), 1)
-    for slot, index in enumerate((ctx, partner)):
-        anchor = jnp.where(
-            lane < half,
-            order[2 * index] * half + lane,
-            order[2 * index + 1] * half + lane - half,
-        )
-        low = jnp.zeros_like(anchor)
-        high = jnp.full_like(anchor, rows * nz * 2)
-        for end in ends:
-            low = jnp.where(end <= anchor, jnp.maximum(low, end), low)
-            high = jnp.where(end > anchor, jnp.minimum(high, end), high)
-        bounds[0:1, slot * rows : (slot + 1) * rows] = low
-        bounds[1:2, slot * rows : (slot + 1) * rows] = high
-
     def ring_copy(h, hop, piece, side):
         source = (z + nz - hop) % nz if side == 0 else (z + hop) % nz
         step = h * depth + hop
@@ -238,6 +216,28 @@
         q_copy(h).start()
     for i in range(1, n_head):
         w_copy(i).start()
+    for copy in tables:
+        copy.wait()
+    ends = []
+    running = jnp.int32(0)
+    for c in range(clips):
+        running = running + lengths[c]
+        ends.append(running)
+    lane = lax.broadcasted_iota(jnp.int32, (1, rows), 1)
+    for slot, index in enumerate((ctx, partner)):
+        anchor = jnp.where(
+            lane < half,
+            order[2 * index] * half + lane,
+            order[2 * index + 1] * half + lane - half,
+        )
+        low = jnp.zeros_like(anchor)
+        high = jnp.full_like(anchor, rows * nz * 2)
+        for end in ends:
+            low = jnp.where(end <= anchor, jnp.maximum(low, end), low)
+            high = jnp.where(end > anchor, jnp.minimum(high, end), high)
+        bounds[0:1, slot * rows : (slot + 1) * rows] = low
+        bounds[1:2, slot * rows : (slot + 1) * rows] = high
+
     total[...] = jnp.zeros_like(total)
     s_send[...] = jnp.zeros_like(s_send)
 
@@ -424,9 +424,10 @@
             for piece in range(2, PIECES):
                 forward(h, d, piece)
 
-        @pl.when(jnp.logical_and(index == 0, core != 0))
-        def _():
-            for other in range(1, heads):
+        for other in range(1, heads):
+
+            @pl.when(jnp.logical_and(index == order_of.index((other, 1)) - 1, core != 0))
+            def _(other=other):
                 send_own(other, range(PIECES))
 
         @pl.when(index == min(finished[0] + 2, steps))

time: 98.8 us -> 99.5 us (level)
  no operation moved by 1% of the time
where the time goes in v12:
time: 99.5 us; the launch traced here: 99.3 us
  Pallas kernels  97.9 us (98%)
    pallas_call x1, Pallas kernels, local(): pl.pallas_call(functools.partial(kernel, nz, n_head), out_shape=pltpu.VME...  97.9 us

profile of v12, /device:TPU:2, one launch (start us, length us, event | category | flops | bytes accessed | tf_op | source)
XLA Modules:
  0.0 99.3 jit_solution(116881193926585331)
XLA Ops:
  0.6 97.9 %shard_map.104 = bf16[256,640]{1,0:T(8,128)(2,1)S(1)} custom-call(bf16[128,384]{1,0:T(8,128)(2,1)} %q_in.1, bf16[128,384]{1,0:T(8,128)(2,1)} %k_in.1, bf16[128,384]{1,0:T(8,128)(2,1)} %v_in.1, bf16[128,384]{1,0:T(8,128)(2,1)} %tq_in.1, bf16[128,384]{1,0:T(8,128)(2,1)} %tk_in.1, bf16[128,384]{1,0:T(8,128)(2,1)} %tv_in.1, bf16[3,128,5120]{2,1,0:T(8,128)(2,1)} %bitcast.1, ...), custom_call_target="tpu_custom_call" | custom-call | flops 3422552064 | bytes 8388608 | tf_op jit(solution)/shard_map/pallas_call | solution.py:480
  98.6 0.8 fusion
